TPU v7x, 32 devices: a whole 2x2x4 slice. The times are simulated.
32 devices in a mesh: dp: 8 (over y, x, core), mp: 4 (over z).
Axes of the slice: x: 2, y: 2, z: 4, core: 2. Of those that a mesh axis runs over, the one named last changes fastest.
Arguments:
- hidden: bfloat16 [4096, 4096], P('dp', 'mp'), may hold values from -50 to 50
- norm_gain: float32 [4096], replicated, may hold values from 0.1 to 1.9
- w_query: bfloat16 [4096, 4096], P(None, 'mp'), may hold values from -0.09375 to 0.09375
- w_out: bfloat16 [4096, 4096], P('mp'), may hold values from -0.09375 to 0.09375
- nb_keys: bfloat16 [64, 128, 4096], P('dp', None, 'mp'), may hold values from -250 to 250
- nb_values: bfloat16 [64, 128, 4096], P('dp', None, 'mp'), may hold values from -10 to 10
- neighbours: int32 [64, 2], P('dp'), may hold values from 0 to 63, as said below
- valid_spans: int32 [8], P('dp'), may hold values from 6 to 8, as said below
Outputs:
- mixed: float32 [4096, 4096], P('dp', 'mp')
Inputs may be any that keep to these rules, and one draw needn't show every extreme that they name: Block ids; block b is stored by index b // 8 of dp, its owner. The two neighbours of a span have different owners. The spans of one index of dp name one owner at most 2 times, and some owner is named exactly 2 times by the live spans of every index of dp. `valid_spans`: some index of dp has all 8 spans live.
All inputs are finite; a program needn't handle non-finite values.
Results may differ from a plain program's by a relative error of at most 0.0066.
Values may be sent and summed in bfloat16 or wider, within the bound.
A program may use at most 128 MiB of HBM per device.

v0:
```python
import math

import jax
import jax.numpy as jnp
from jax import lax
from jax.sharding import PartitionSpec as P

HS = 128
SPAN = 64
NBR = 128


eps = 1e-05


def shifted(block, axis, distance):
    devices = range(lax.axis_size(axis))
    route = [(i - distance, i) for i in devices if i - distance in devices]
    return lax.ppermute(block, axis, route)


def partial_attention(query_rows, key_rows, value_rows):
    inner_width = key_rows.shape[-1]
    head_count = inner_width // HS
    query_heads = query_rows.reshape(query_rows.shape[:-1] + (head_count, HS))
    key_heads = key_rows.reshape(key_rows.shape[:-1] + (head_count, HS))
    value_heads = value_rows.reshape(value_rows.shape[:-1] + (head_count, HS))
    factor = 1.0 / math.sqrt(HS)
    scores = (
        jnp.einsum(
            "...qhd,...khd->...qhk", query_heads, key_heads, preferred_element_type=jnp.float32
        )
        * factor
    )
    score_top = jnp.max(scores, axis=-1)
    weights = jnp.exp(scores - score_top[..., None])
    weight_sum = jnp.sum(weights, axis=-1)
    summed = jnp.einsum(
        "...qhk,...khd->...qhd",
        weights.astype(jnp.bfloat16),
        value_heads,
        preferred_element_type=jnp.float32,
    )
    part_out = (summed / weight_sum[..., None]).astype(jnp.bfloat16)
    return (part_out.reshape(part_out.shape[:-2] + (inner_width,)), score_top, weight_sum)


def combine(part_out, score_top, weight_sum):
    head_count = score_top.shape[-1]
    best_score = jnp.max(score_top, axis=1, keepdims=True)
    mix_weight = jnp.exp(score_top - best_score) * weight_sum
    widened = part_out.reshape(part_out.shape[:-1] + (head_count, HS)).astype(jnp.float32)
    merged = (
        jnp.sum(widened * mix_weight[..., None], axis=1) / jnp.sum(mix_weight, axis=1)[..., None]
    )
    return merged.reshape(merged.shape[:-2] + (head_count * HS,)).astype(jnp.bfloat16)


def shards(hidden, norm_gain, w_query, w_out, nb_keys, nb_values, neighbours, valid_spans):
    tok_rows = hidden.shape[0]
    span_dev = tok_rows // SPAN
    stored = nb_keys.shape[0]
    inner_width = w_query.shape[1]
    peer_count = lax.axis_size("dp")
    most_slots = max(2, (2 * span_dev + peer_count - 1) // peer_count)
    widened = lax.all_gather(hidden, "mp", axis=1, tiled=True).astype(jnp.float32)
    normed = (
        widened * lax.rsqrt(jnp.mean(widened * widened, axis=1, keepdims=True) + eps) * norm_gain
    ).astype(jnp.bfloat16)
    queries = jnp.dot(normed, w_query, preferred_element_type=jnp.float32).astype(jnp.bfloat16)
    following = shifted(queries[: SPAN - 1], "dp", -1)
    grouped = jnp.concatenate([queries[SPAN - 1 :], following], axis=0).reshape(
        span_dev, SPAN, inner_width
    )
    live_span = jnp.arange(span_dev, dtype=jnp.int32) < valid_spans[0]
    owners = (neighbours // stored).reshape(-1)
    slot_ids = (neighbours % stored).reshape(-1)
    is_live = jnp.repeat(live_span, 2)
    req_order = jnp.arange(owners.shape[0], dtype=jnp.int32)
    earlier = (
        (owners[:, None] == owners[None, :])
        & is_live[None, :]
        & (req_order[None, :] < req_order[:, None])
    )
    slot_rank = jnp.minimum(jnp.sum(earlier.astype(jnp.int32), axis=1), most_slots - 1)
    target = jnp.where(is_live, owners * most_slots + slot_rank, -1)
    slot_match = target[:, None] == jnp.arange(peer_count * most_slots, dtype=jnp.int32)[None, :]
    filled = jnp.any(slot_match, axis=0)
    request_table = jnp.where(
        filled, jnp.sum(jnp.where(slot_match, slot_ids[:, None], 0), axis=0), -1
    )
    request_table = request_table.reshape(peer_count, most_slots)
    safe_ids = jnp.maximum(
        lax.all_to_all(request_table, "dp", split_axis=0, concat_axis=0, tiled=True), 0
    )
    keys_back = lax.all_to_all(nb_keys[safe_ids], "dp", split_axis=0, concat_axis=0, tiled=True)
    values_back = lax.all_to_all(nb_values[safe_ids], "dp", split_axis=0, concat_axis=0, tiled=True)
    key_rows = keys_back[owners, slot_rank].reshape(span_dev, 2, NBR, inner_width)
    value_rows = values_back[owners, slot_rank].reshape(span_dev, 2, NBR, inner_width)
    part_out, score_top, weight_sum = partial_attention(grouped[:, None], key_rows, value_rows)
    merged = combine(part_out, score_top, weight_sum)
    merged = jnp.where(live_span[:, None, None], merged, jnp.zeros_like(merged))
    flat_rows = merged.reshape(tok_rows, inner_width)
    previous = shifted(flat_rows[tok_rows - SPAN + 1 :], "dp", 1)
    placed = jnp.concatenate([previous, flat_rows[: tok_rows - SPAN + 1]], axis=0)
    head_terms = jnp.dot(placed, w_out, preferred_element_type=jnp.float32)
    summed = lax.psum_scatter(head_terms, "mp", scatter_dimension=1, tiled=True)
    return hidden.astype(jnp.float32) + summed


def solution(mesh):
    placed = (
        P("dp", "mp"),
        P(),
        P(None, "mp"),
        P("mp", None),
        P("dp", None, "mp"),
        P("dp", None, "mp"),
        P("dp", None),
        P("dp"),
    )
    return jax.shard_map(
        shards, mesh=mesh, in_specs=placed, out_specs=P("dp", "mp"), check_vma=False
    )
```

profile of v0, /device:TPU:8, one launch (start us, length us, event | category | flops | bytes accessed | tf_op | source)
XLA Modules:
  0.0 320.1 jit_solution(150078188198173860)
XLA Ops:
  6.5 0.7 all-gather.2.cloned.1.call-update
  7.9 0.1 broadcast_in_dim.58
  8.0 0.1 reshape.140
  8.1 0.7 and_select_fusion
  8.8 0.1 copy.62
  8.9 0.1 broadcast_in_dim.60
  8.9 0.1 copy.61
  9.0 0.1 reshape.141
  9.1 0.2 convert_reduce_fusion
  9.3 0.1 fusion.24
  9.4 0.1 select_reduce_fusion
  9.5 0.1 select_n.72
  9.6 8.2 %all_to_all.16 = s32[8,1,2]{2,1,0:T(1,128)S(1)} all-to-all(s32[8,1,2]{2,1,0:T(1,128)S(1)} %bitcast.50), channel_id=1, replica_groups=mesh['dp'=8,'mp'=4] {'dp'}, dimensions={0} | all-to-all | bytes 128 | tf_op jit(solution)/shard_map/all_to_all | solution.py:94
  17.8 0.1 reshape.145
  17.9 2.7 gather_fusion.2
  20.6 4.7 %all-to-all-start.2 = ((bf16[8,2,128,1024]{3,2,1,0:T(8,128)(2,1)}), bf16[8,2,128,1024]{3,2,1,0:T(8,128)(2,1)}, u32[]{:S(2)}, u32[]{:S(2)}) async-start(bf16[8,2,128,1024]{3,2,1,0:T(8,128)(2,1)} %bitcast.46), calls=%async_computation.2 | async-start | bytes 8388608 | tf_op jit(solution)/shard_map/all_to_all | solution.py:96
  25.4 2.8 gather_fusion
  28.1 46.3 %all-to-all-done.2 = bf16[8,2,128,1024]{3,2,1,0:T(8,128)(2,1)} async-done(((bf16[8,2,128,1024]{3,2,1,0:T(8,128)(2,1)}), bf16[8,2,128,1024]{3,2,1,0:T(8,128)(2,1)}, u32[]{:S(2)}, u32[]{:S(2)}) %all-to-all-start.2) | async-done | bytes 4194336 | tf_op jit(solution)/shard_map/all_to_all | solution.py:96
  74.5 4.7 %all-to-all-start.1 = ((bf16[8,2,128,1024]{3,2,1,0:T(8,128)(2,1)}), bf16[8,2,128,1024]{3,2,1,0:T(8,128)(2,1)}, u32[]{:S(2)}, u32[]{:S(2)}) async-start(bf16[8,2,128,1024]{3,2,1,0:T(8,128)(2,1)} %bitcast.45), calls=%async_computation.1 | async-start | bytes 8388608 | tf_op jit(solution)/shard_map/all_to_all | solution.py:97
  79.2 0.1 reshape.142
  79.3 0.1 broadcast_in_dim.32
  79.4 0.1 broadcast_in_dim.56
  79.4 8.8 %all-gather.2.cloned.1.call-done = bf16[512,4096]{1,0:T(8,128)(2,1)} async-done(((bf16[512,1024]{1,0:T(8,128)(2,1)}), bf16[512,4096]{1,0:T(8,128)(2,1)}) %all-gather.2.cloned.1.call-update) | async-done | bytes 4194320 | tf_op jit(solution)/shard_map/all_gather | solution.py:66
  88.2 3.2 %fusion = f32[512]{0:T(512)S(1)} fusion(bf16[512,4096]{1,0:T(8,128)(2,1)} %all-gather.2.cloned.1.call-done), kind=kLoop, calls=%fused_computation.6 | loop fusion | flops 6290944 | bytes 4196352 | tf_op jit(solution)/shard_map/reduce_sum | solution.py:68
  91.5 0.2 copy-done.5
  91.7 7.2 %fusion.14 = bf16[512,1024]{1,0:T(8,128)(2,1)S(1)} fusion(bf16[4096,1024]{1,0:T(8,128)(2,1)} %param.10, bf16[512,4096]{1,0:T(8,128)(2,1)S(1)} %copy-done.5, f32[4096]{0:T(1024)S(1)} %copy-done.7, f32[512]{0:T(512)S(1)} %add_rsqrt_fusion), kind=kOutput, calls=%fused_computation.26 | convolution fusion | flops 4303880192 | bytes 13649920 | tf_op jit(solution)/shard_map/dot_general | solution.py:70
  98.8 1.3 collective-permute-start
  100.2 5.0 %gather_fusion.3 = bf16[16,128,1024]{2,1,0:T(8,128)(2,1)} fusion(bf16[8,2,128,1024]{3,2,1,0:T(8,128)(2,1)} %all-to-all-done.2, s32[16]{0:T(128)S(1)} %fusion.31), kind=kCustom, calls=%fused_computation.3 | custom fusion | bytes 8388736 | tf_op jit(solution)/shard_map/gather | solution.py:98
  105.1 6.4 %copy.66 = bf16[16,128,1024]{1,2,0:T(8,128)(2,1)} copy(bf16[16,128,1024]{2,1,0:T(8,128)(2,1)} %gather_fusion.3) | data formatting | bytes 8388608 | tf_op jit(solution)/shard_map/gather | solution.py:98
  111.5 16.8 %all-to-all-done.1 = bf16[8,2,128,1024]{3,2,1,0:T(8,128)(2,1)} async-done(((bf16[8,2,128,1024]{3,2,1,0:T(8,128)(2,1)}), bf16[8,2,128,1024]{3,2,1,0:T(8,128)(2,1)}, u32[]{:S(2)}, u32[]{:S(2)}) %all-to-all-start.1) | async-done | bytes 4194336 | tf_op jit(solution)/shard_map/all_to_all | solution.py:97
  128.3 5.0 %gather_fusion.1 = bf16[16,128,1024]{2,1,0:T(8,128)(2,1)} fusion(bf16[8,2,128,1024]{3,2,1,0:T(8,128)(2,1)} %all-to-all-done.1, s32[16]{0:T(128)S(1)} %fusion.31), kind=kCustom, calls=%fused_computation.1 | custom fusion | bytes 8388736 | tf_op jit(solution)/shard_map/gather | solution.py:99
  133.3 6.4 %copy.65 = bf16[16,128,1024]{1,2,0:T(8,128)(2,1)} copy(bf16[16,128,1024]{2,1,0:T(8,128)(2,1)} %gather_fusion.1) | data formatting | bytes 8388608 | tf_op jit(solution)/shard_map/gather | solution.py:99
  139.6 0.2 slice.24
  139.9 0.1 maximum_bitcast_fusion
  140.0 0.3 copy.80
  140.4 1.5 copy-done.2
  141.8 1.4 bitcast_reduce_fusion.1
  143.3 3.6 %bitcast_reduce_fusion = (f32[8,64,8]{1,2,0:T(8,128)S(1)}, f32[8,2,64,8]{2,1,3,0:T(2,128)S(1)}, bf16[8,2,64,8,128]{4,2,1,3,0:T(8,128)(2,1)S(1)}) fusion(f32[8,8,2,128,64]{3,4,2,1,0:T(8,128)S(1)} %get-tuple-element.13, f32[8,2,64,8]{2,1,3,0:T(2,128)S(1)} %get-tuple-element.12), kind=kLoop, calls=%fused_computation.12 | loop fusion | flops 5230592 | bytes 6373376 | tf_op jit(solution)/shard_map/reduce_max | solution.py:50
  146.9 0.1 fusion.33
  147.1 3.6 %multiply_reduce_fusion = f32[8,64,8,128]{3,1,2,0:T(8,128)S(1)} fusion(f32[8,2,64,8]{2,3,1,0:T(8,128)S(1)} %copy.72, f32[8,2,64,8]{2,3,1,0:T(8,128)S(1)} %copy.71, bf16[8,2,128,8,128]{2,4,3,1,0:T(8,128)(2,1)S(1)} %bitcast.48, bf16[8,2,64,8,128]{4,2,1,3,0:T(8,128)(2,1)S(1)} %get-tuple-element.9), kind=kOutput, calls=%fused_computation.18 | convolution fusion | flops 273154048 | bytes 8454144 | tf_op jit(solution)/shard_map/...qhk,...khd->...qhd/dot_general | solution.py:38
  150.6 0.7 divide_convert_fusion
  151.4 0.7 copy.73
  152.1 0.2 bitcast_select_fusion
  152.3 1.3 collective-permute-start.1
  153.7 0.9 collective-permute-done.1
  154.6 6.8 %fusion.17 = f32[512,4096]{1,0:T(8,128)} fusion(bf16[1024,4096]{1,0:T(8,128)(2,1)S(1)} %bitcast.52, bf16[449,1024]{1,0:T(8,128)(2,1)S(1)} %slice.27, bf16[63,1024]{1,0:T(8,128)(2,1)S(1)} %collective-permute-done.1), kind=kOutput, calls=%fused_computation.30 | convolution fusion | flops 4297064448 | bytes 17825792 | tf_op jit(solution)/shard_map/dot_general | solution.py:106
  161.4 148.5 %reduce-scatter.2.cloned.1.call-done = f32[512,1024]{1,0:T(8,128)} async-done(((f32[512,4096]{1,0:T(8,128)}), f32[512,1024]{1,0:T(8,128)}) %reduce-scatter.2.cloned.1.call-update) | async-done | bytes 2097168 | tf_op jit(solution)/shard_map/reduce_scatter | solution.py:107
  309.9 3.4 %convert_add_fusion = f32[512,1024]{1,0:T(8,128)} fusion(f32[512,1024]{1,0:T(8,128)} %reduce-scatter.2.cloned.1.call-done, bf16[512,1024]{1,0:T(8,128)(2,1)S(1)} %copy-done.4), kind=kLoop, calls=%fused_computation.25 | loop fusion | flops 1048576 | bytes 5242880 | tf_op jit(solution)/shard_map/add | solution.py:108
  (36 shorter events, 0.4 us)
Async XLA Ops:
  6.5 11.3 %copy-start = (bf16[8,128,1024]{2,1,0:T(8,128)(2,1)S(1)}, bf16[8,128,1024]{2,1,0:T(8,128)(2,1)}, u32[]{:S(2)}) copy-start(bf16[8,128,1024]{2,1,0:T(8,128)(2,1)} %param.12) | copy-start | bytes 6291460
  6.5 81.7 %all-gather.2.cloned.1.call-start = ((), (), s32[]{:S(2)}) async-start(), calls=%async_computation.4 | async-start | bytes 5242880 | tf_op jit(solution)/shard_map/all_gather | solution.py:66
  20.6 4.7 %copy-start.3 = (bf16[8,128,1024]{2,1,0:T(8,128)(2,1)S(1)}, bf16[8,128,1024]{2,1,0:T(8,128)(2,1)}, u32[]{:S(2)}) copy-start(bf16[8,128,1024]{2,1,0:T(8,128)(2,1)} %param.13) | copy-start | bytes 6291460
  20.6 53.9 %all-to-all-start.2 = ((bf16[8,2,128,1024]{3,2,1,0:T(8,128)(2,1)}), bf16[8,2,128,1024]{3,2,1,0:T(8,128)(2,1)}, u32[]{:S(2)}, u32[]{:S(2)}) async-start(bf16[8,2,128,1024]{3,2,1,0:T(8,128)(2,1)} %bitcast.46), calls=%async_computation.2 | async-start | bytes 8388608 | tf_op jit(solution)/shard_map/all_to_all | solution.py:96
  74.5 17.0 %copy-start.7 = (f32[4096]{0:T(1024)S(1)}, f32[4096]{0:T(1024)}, u32[]{:S(2)}) copy-start(f32[4096]{0:T(1024)} %param.9) | copy-start | bytes 49156
  74.5 53.8 %all-to-all-start.1 = ((bf16[8,2,128,1024]{3,2,1,0:T(8,128)(2,1)}), bf16[8,2,128,1024]{3,2,1,0:T(8,128)(2,1)}, u32[]{:S(2)}, u32[]{:S(2)}) async-start(bf16[8,2,128,1024]{3,2,1,0:T(8,128)(2,1)} %bitcast.45), calls=%async_computation.1 | async-start | bytes 8388608 | tf_op jit(solution)/shard_map/all_to_all | solution.py:97
  79.2 230.7 %reduce-scatter.2.cloned.1.call-start = ((), (), s32[]{:S(2)}) async-start(), calls=%async_computation.5 | async-start | bytes 10485760 | tf_op jit(solution)/shard_map/reduce_scatter | solution.py:107
  88.2 3.4 %copy-start.5 = (bf16[512,4096]{1,0:T(8,128)(2,1)S(1)}, bf16[512,4096]{1,0:T(8,128)(2,1)}, u32[]{:S(2)}) copy-start(bf16[512,4096]{1,0:T(8,128)(2,1)} %all-gather.2.cloned.1.call-done) | copy-start | bytes 12582916
  98.8 41.0 %collective-permute-start = (bf16[63,1024]{1,0:T(8,128)(2,1)S(1)}, bf16[63,1024]{1,0:T(8,128)(2,1)S(1)}, u32[]{:S(2)}, u32[]{:S(2)}) collective-permute-start(bf16[63,1024]{1,0:T(8,128)(2,1)S(1)} %slice.25), channel_id=1, source_target_pairs={{4,0},{8,4},{12,8},{16,12},{20,16},{24,20},{28,24},{5,1},{9,5},{13... | collective-permute-start | bytes 387080 | tf_op jit(solution)/shard_map/ppermute | solution.py:19
  139.6 2.2 copy-start.2
  143.3 3.8 %copy-start.6 = (bf16[16,128,1024]{1,2,0:T(8,128)(2,1)S(1)}, bf16[16,128,1024]{1,2,0:T(8,128)(2,1)}, u32[]{:S(2)}) copy-start(bf16[16,128,1024]{1,2,0:T(8,128)(2,1)} %copy.65) | copy-start | bytes 12582916
  147.0 7.5 %slice-start = ((s8[8388608]{0:T(1024)(128)(4,1)}), s8[4194304]{0:T(1024)(128)(4,1)S(1)}, s32[]{:S(2)}) async-start(s8[8388608]{0:T(1024)(128)(4,1)} %bitcast.51), calls=%async_computation.6 | async-start | bytes 8388608
  147.0 7.5 %slice-start.1 = ((s8[8388608]{0:T(1024)(128)(4,1)}), s8[4194304]{0:T(1024)(128)(4,1)S(1)}, s32[]{:S(2)}) async-start(s8[8388608]{0:T(1024)(128)(4,1)} %bitcast.51), calls=%async_computation.7 | async-start | bytes 8388608
  152.3 2.3 collective-permute-start.1
  161.4 148.5 %copy-start.4 = (bf16[512,1024]{1,0:T(8,128)(2,1)S(1)}, bf16[512,1024]{1,0:T(8,128)(2,1)}, u32[]{:S(2)}) copy-start(bf16[512,1024]{1,0:T(8,128)(2,1)} %param.8) | copy-start | bytes 3145732
  161.4 151.8 %copy-start.1 = (bf16[8,128,1024]{2,1,0:T(8,128)(2,1)S(1)}, bf16[8,128,1024]{2,1,0:T(8,128)(2,1)}, u32[]{:S(2)}) copy-start(bf16[8,128,1024]{2,1,0:T(8,128)(2,1)} %param.12) | copy-start | bytes 6291460
Sparse Core Ops, SparseCore 0:
  8.9 79.2 all-gather.1
  161.5 148.3 reduce-scatter.1
where the time goes:
time: 323 us; the launch traced here: 320 us
  waiting for transfers between devices  222 us (69%)
  local copies, waits for them, and re-layouts  32.2 us (10%)
  matrix products  19 us (6%)
  between operations  14.3 us (4%)
  other arithmetic  12.4 us (4%)
  starting transfers between devices  12 us (4%)
  blocking collectives  8.18 us (3%)
    reduce_scatter x1, waiting for transfers between devices, shards(): summed = lax.psum_scatter(head_terms, 'mp', scatter_dimension=1, tiled=True)  148 us
    all_to_all x1, waiting for transfers between devices, shards(): lax.all_to_all(nb_keys[safe_ids], 'dp', split_axis=0, concat_axis=0, tile...  46.3 us
    all_to_all x1, waiting for transfers between devices, shards(): lax.all_to_all(nb_values[safe_ids], 'dp', split_axis=0, concat_axis=0, ti...  16.8 us
    gather x2, local copies, waits for them, and re-layouts, shards(): values_back[owners, slot_rank].reshape(span_dev, 2, NBR, inner_width)  11.4 us
    gather x2, local copies, waits for them, and re-layouts, shards(): keys_back[owners, slot_rank].reshape(span_dev, 2, NBR, inner_width)  11.3 us
    all_gather x1, waiting for transfers between devices, shards(): lax.all_gather(hidden, 'mp', axis=1, tiled=True).astype(jnp.float32)  8.76 us
    all_to_all x1, blocking collectives, shards(): lax.all_to_all(request_table, 'dp', split_axis=0, concat_axis=0, tiled=True)  8.18 us
    dot_general x1, matrix products, shards(): jnp.dot(normed, w_query, preferred_element_type=jnp.float32)  7.17 us
  transfers between devices with their start and end apart: 6, of which 5 were waited for; matrix products, arithmetic and copies ran while one was open for 13% of the time, Pallas kernels for 0%

commit v1 on v0

v1 whole, which is shorter than its diff:
```python
import functools
import math

import jax
import jax.numpy as jnp
from jax import lax
from jax.experimental import pallas as pl
from jax.experimental.pallas import tpu as pltpu
from jax.sharding import PartitionSpec as P

HS = 128
SPAN = 64
NBR = 128


eps = 1e-05


def shifted(block, axis, distance):
    devices = range(lax.axis_size(axis))
    route = [(i - distance, i) for i in devices if i - distance in devices]
    return lax.ppermute(block, axis, route)


def attention_kernel(slots, live, q_ref, k0_ref, k1_ref, v0_ref, v1_ref, out_ref):
    span = pl.program_id(0)
    factor = 1.0 / math.sqrt(HS)
    keep = live[span] > 0
    for head in range(q_ref.shape[1] // HS):
        cols = slice(head * HS, (head + 1) * HS)
        query = q_ref[:, cols]
        keys = jnp.concatenate([k0_ref[0, :, cols], k1_ref[0, :, cols]], axis=0)
        values = jnp.concatenate([v0_ref[0, :, cols], v1_ref[0, :, cols]], axis=0)
        scores = (
            lax.dot_general(
                query, keys, (((1,), (1,)), ((), ())), preferred_element_type=jnp.float32
            )
            * factor
        )
        weights = jnp.exp(scores - jnp.max(scores, axis=1, keepdims=True))
        total = jnp.sum(weights, axis=1, keepdims=True)
        summed = jnp.dot(
            weights.astype(jnp.bfloat16), values, preferred_element_type=jnp.float32
        )
        merged = summed / total
        out_ref[:, cols] = jnp.where(keep, merged, 0.0).astype(jnp.bfloat16)


def attention(slots, live, grouped, key_rows, value_rows):
    rows, width = grouped.shape
    spans = rows // SPAN

    def block(which):
        return pl.BlockSpec(
            (1, NBR, width), lambda span, slots, live: (slots[2 * span + which], 0, 0)
        )

    token_block = pl.BlockSpec((SPAN, width), lambda span, slots, live: (span, 0))
    return pl.pallas_call(
        attention_kernel,
        grid_spec=pltpu.PrefetchScalarGridSpec(
            num_scalar_prefetch=2,
            grid=(spans,),
            in_specs=[token_block, block(0), block(1), block(0), block(1)],
            out_specs=token_block,
        ),
        out_shape=jax.ShapeDtypeStruct((rows, width), jnp.bfloat16),
        compiler_params=pltpu.CompilerParams(vmem_limit_bytes=24 * 2**20),
        cost_estimate=pl.CostEstimate(
            flops=8 * rows * NBR * width,
            bytes_accessed=4 * rows * width + 8 * spans * NBR * width,
            transcendentals=2 * rows * NBR * width // HS,
        ),
    )(slots, live, grouped, key_rows, key_rows, value_rows, value_rows)


def shards(hidden, norm_gain, w_query, w_out, nb_keys, nb_values, neighbours, valid_spans):
    tok_rows = hidden.shape[0]
    span_dev = tok_rows // SPAN
    stored = nb_keys.shape[0]
    inner_width = w_query.shape[1]
    peer_count = lax.axis_size("dp")
    most_slots = max(2, (2 * span_dev + peer_count - 1) // peer_count)
    widened = lax.all_gather(hidden, "mp", axis=1, tiled=True).astype(jnp.float32)
    normed = (
        widened * lax.rsqrt(jnp.mean(widened * widened, axis=1, keepdims=True) + eps) * norm_gain
    ).astype(jnp.bfloat16)
    queries = jnp.dot(normed, w_query, preferred_element_type=jnp.float32).astype(jnp.bfloat16)
    following = shifted(queries[: SPAN - 1], "dp", -1)
    grouped = jnp.concatenate([queries[SPAN - 1 :], following], axis=0)
    live_span = jnp.arange(span_dev, dtype=jnp.int32) < valid_spans[0]
    owners = (neighbours // stored).reshape(-1)
    slot_ids = (neighbours % stored).reshape(-1)
    is_live = jnp.repeat(live_span, 2)
    req_order = jnp.arange(owners.shape[0], dtype=jnp.int32)
    earlier = (
        (owners[:, None] == owners[None, :])
        & is_live[None, :]
        & (req_order[None, :] < req_order[:, None])
    )
    slot_rank = jnp.minimum(jnp.sum(earlier.astype(jnp.int32), axis=1), most_slots - 1)
    target = jnp.where(is_live, owners * most_slots + slot_rank, -1)
    slot_match = target[:, None] == jnp.arange(peer_count * most_slots, dtype=jnp.int32)[None, :]
    filled = jnp.any(slot_match, axis=0)
    request_table = jnp.where(
        filled, jnp.sum(jnp.where(slot_match, slot_ids[:, None], 0), axis=0), -1
    )
    request_table = request_table.reshape(peer_count, most_slots)
    safe_ids = jnp.maximum(
        lax.all_to_all(request_table, "dp", split_axis=0, concat_axis=0, tiled=True), 0
    )
    keys_back = lax.all_to_all(nb_keys[safe_ids], "dp", split_axis=0, concat_axis=0, tiled=True)
    values_back = lax.all_to_all(nb_values[safe_ids], "dp", split_axis=0, concat_axis=0, tiled=True)
    flat_slots = (peer_count * most_slots, NBR, inner_width)
    merged = attention(
        owners * most_slots + slot_rank,
        live_span.astype(jnp.int32),
        grouped,
        keys_back.reshape(flat_slots),
        values_back.reshape(flat_slots),
    )
    previous = shifted(merged[tok_rows - SPAN + 1 :], "dp", 1)
    placed = jnp.concatenate([previous, merged[: tok_rows - SPAN + 1]], axis=0)
    head_terms = jnp.dot(placed, w_out, preferred_element_type=jnp.float32).astype(jnp.bfloat16)
    summed = lax.psum_scatter(head_terms, "mp", scatter_dimension=1, tiled=True)
    return hidden.astype(jnp.float32) + summed.astype(jnp.float32)


def solution(mesh):
    placed = (
        P("dp", "mp"),
        P(),
        P(None, "mp"),
        P("mp", None),
        P("dp", None, "mp"),
        P("dp", None, "mp"),
        P("dp", None),
        P("dp"),
    )
    return jax.shard_map(
        shards, mesh=mesh, in_specs=placed, out_specs=P("dp", "mp"), check_vma=False
    )
```

time: 323 us -> 252 us (0.78)
  waiting for transfers between devices: 222 us -> 163 us
  local copies, waits for them, and re-layouts: 32.2 us -> 8.37 us
  Pallas kernels: 0 us -> 18.6 us
  other arithmetic: 12.4 us -> 7.36 us
    reduce_scatter x1, waiting for transfers between devices: 148 us -> 80.1 us  [shards(): summed = lax.psum_scatter(head_terms, 'mp', scatter_dimension=1, tiled=True)]
    gather x4 -> x0, local copies, waits for them, and re-layouts: 22.7 us -> none  [the longest x2 11.4 us: shards(): values_back[owners, slot_rank].reshape(span_dev, 2, NBR, inner_width)]
    pallas_call x0 -> x1, Pallas kernels: none -> 18.6 us  [attention(): pl.pallas_call(attention_kernel, grid_spec=pltpu.PrefetchScalarGridSpec(n...]
    all_to_all x1, waiting for transfers between devices: 16.8 us -> 26 us  [shards(): lax.all_to_all(nb_values[safe_ids], 'dp', split_axis=0, concat_axis=0, ti...]
    reduce_max x1 -> x0, other arithmetic: 3.58 us -> none  [combine(): best_score = jnp.max(score_top, axis=1, keepdims=True)]
    dot_general x3 -> x1, matrix products: 11.8 us -> 9.53 us  [shards(): jnp.dot(placed, w_out, preferred_element_type=jnp.float32)]
  transfers between devices with their start and end apart: 6 -> 6, of which waited for: 5 -> 6; matrix products, arithmetic and copies ran while one was open for 13% -> 8% of each run, Pallas kernels for 0% -> 0%
where the time goes in v1:
time: 252 us; the launch traced here: 249 us
  waiting for transfers between devices  163 us (65%)
  Pallas kernels  18.6 us (7%)
  matrix products  16.7 us (7%)
  between operations  14.2 us (6%)
  starting transfers between devices  12.8 us (5%)
  local copies, waits for them, and re-layouts  8.37 us (3%)
  blocking collectives  8.18 us (3%)
  other arithmetic  7.36 us (3%)
    reduce_scatter x1, waiting for transfers between devices, shards(): summed = lax.psum_scatter(head_terms, 'mp', scatter_dimension=1, tiled=True)  80.1 us
    all_to_all x1, waiting for transfers between devices, shards(): lax.all_to_all(nb_keys[safe_ids], 'dp', split_axis=0, concat_axis=0, tile...  44.8 us
    all_to_all x1, waiting for transfers between devices, shards(): lax.all_to_all(nb_values[safe_ids], 'dp', split_axis=0, concat_axis=0, ti...  26 us
    pallas_call x1, Pallas kernels, attention(): pl.pallas_call(attention_kernel, grid_spec=pltpu.PrefetchScalarGridSpec(n...  18.6 us
    dot_general x1, matrix products, shards(): jnp.dot(placed, w_out, preferred_element_type=jnp.float32)  9.53 us
    all_gather x1, waiting for transfers between devices, shards(): lax.all_gather(hidden, 'mp', axis=1, tiled=True).astype(jnp.float32)  9.08 us
    all_to_all x1, blocking collectives, shards(): lax.all_to_all(request_table, 'dp', split_axis=0, concat_axis=0, tiled=True)  8.18 us
    dot_general x1, matrix products, shards(): jnp.dot(normed, w_query, preferred_element_type=jnp.float32)  7.17 us
  transfers between devices with their start and end apart: 6, of which 6 were waited for; matrix products, arithmetic and copies ran while one was open for 8% of the time, Pallas kernels for 0%

profile of v1, /device:TPU:8, one launch (start us, length us, event | category | flops | bytes accessed | tf_op | source)
XLA Modules:
  0.0 249.5 jit_solution(10049583205279414568)
XLA Ops:
  6.5 0.0 copy-start
  6.5 0.0 all-gather.2.cloned.1.call-start
  6.5 0.7 all-gather.2.cloned.1.call-update
  7.3 0.7 and_select_fusion
  7.9 0.1 copy.16
  8.0 0.1 reshape.73
  8.8 0.1 broadcast_in_dim.30
  8.9 0.1 and.24
  8.9 0.1 copy.17
  9.0 0.1 broadcast_in_dim.32
  9.1 0.2 convert_reduce_fusion
  9.3 0.1 fusion.13
  9.4 0.1 select_reduce_fusion
  9.5 0.1 select_n.45
  9.6 8.2 %all_to_all.16 = s32[8,1,2]{2,1,0:T(1,128)S(1)} all-to-all(s32[8,1,2]{2,1,0:T(1,128)S(1)} %bitcast.12), channel_id=1, replica_groups=mesh['dp'=8,'mp'=4] {'dp'}, dimensions={0} | all-to-all | bytes 128 | tf_op jit(solution)/shard_map/all_to_all | solution.py:110
  17.8 0.1 reshape.78
  17.9 0.0 copy-done
  17.9 2.8 %gather_fusion = bf16[16,128,1024]{2,1,0:T(8,128)(2,1)} fusion(bf16[8,128,1024]{2,1,0:T(8,128)(2,1)S(1)} %copy-done, s32[1024]{0:T(1024)S(1)} %pad_clamp_fusion), kind=kCustom, calls=%fused_computation | custom fusion | bytes 8388672 | tf_op jit(solution)/shard_map/gather | solution.py:112
  20.7 4.5 %all-to-all-start.1 = ((bf16[8,2,128,1024]{3,2,1,0:T(8,128)(2,1)}), bf16[8,2,128,1024]{3,2,1,0:T(8,128)(2,1)}, u32[]{:S(2)}, u32[]{:S(2)}) async-start(bf16[8,2,128,1024]{3,2,1,0:T(8,128)(2,1)} %bitcast.11), calls=%async_computation.1 | async-start | bytes 8388608 | tf_op jit(solution)/shard_map/all_to_all | solution.py:112
  25.2 4.4 %gather_fusion.1 = bf16[16,128,1024]{2,1,0:T(8,128)(2,1)} fusion(bf16[8,128,1024]{2,1,0:T(8,128)(2,1)} %param.13, s32[1024]{0:T(1024)S(1)} %pad_clamp_fusion), kind=kCustom, calls=%fused_computation.1 | custom fusion | bytes 8388672 | tf_op jit(solution)/shard_map/gather | solution.py:113
  29.6 44.8 %all-to-all-done.1 = bf16[8,2,128,1024]{3,2,1,0:T(8,128)(2,1)} async-done(((bf16[8,2,128,1024]{3,2,1,0:T(8,128)(2,1)}), bf16[8,2,128,1024]{3,2,1,0:T(8,128)(2,1)}, u32[]{:S(2)}, u32[]{:S(2)}) %all-to-all-start.1) | async-done | bytes 4194336 | tf_op jit(solution)/shard_map/all_to_all | solution.py:112
  74.3 0.0 copy-start.3
  74.3 4.7 %all-to-all-start.2 = ((bf16[8,2,128,1024]{3,2,1,0:T(8,128)(2,1)}), bf16[8,2,128,1024]{3,2,1,0:T(8,128)(2,1)}, u32[]{:S(2)}, u32[]{:S(2)}) async-start(bf16[8,2,128,1024]{3,2,1,0:T(8,128)(2,1)} %bitcast.10), calls=%async_computation.2 | async-start | bytes 8388608 | tf_op jit(solution)/shard_map/all_to_all | solution.py:113
  79.1 0.0 reduce-scatter.2.cloned.1.call-start
  79.1 9.1 %all-gather.2.cloned.1.call-done = bf16[512,4096]{1,0:T(8,128)(2,1)} async-done(((bf16[512,1024]{1,0:T(8,128)(2,1)}), bf16[512,4096]{1,0:T(8,128)(2,1)}) %all-gather.2.cloned.1.call-update) | async-done | bytes 4194320 | tf_op jit(solution)/shard_map/all_gather | solution.py:84
  88.2 0.0 copy-start.1
  88.2 3.2 %fusion = f32[512]{0:T(512)S(1)} fusion(bf16[512,4096]{1,0:T(8,128)(2,1)} %all-gather.2.cloned.1.call-done), kind=kLoop, calls=%fused_computation.4 | loop fusion | flops 6290944 | bytes 4196352 | tf_op jit(solution)/shard_map/reduce_sum | solution.py:86
  91.4 0.0 copy-done.3
  91.5 0.2 copy-done.1
  91.7 7.2 %fusion.7 = bf16[512,1024]{1,0:T(8,128)(2,1)S(1)} fusion(bf16[4096,1024]{1,0:T(8,128)(2,1)} %param.10, bf16[512,4096]{1,0:T(8,128)(2,1)S(1)} %copy-done.1, f32[4096]{0:T(1024)S(1)} %copy-done.3, f32[512]{0:T(512)S(1)} %add_rsqrt_fusion), kind=kOutput, calls=%fused_computation.12 | convolution fusion | flops 4303880192 | bytes 13649920 | tf_op jit(solution)/shard_map/dot_general | solution.py:88
  98.9 1.3 collective-permute-start
  100.2 0.2 slice.20
  100.4 1.7 collective-permute-done
  102.1 0.1 pad_maximum_fusion.q_ref
  102.2 26.0 %all-to-all-done.2 = bf16[8,2,128,1024]{3,2,1,0:T(8,128)(2,1)} async-done(((bf16[8,2,128,1024]{3,2,1,0:T(8,128)(2,1)}), bf16[8,2,128,1024]{3,2,1,0:T(8,128)(2,1)}, u32[]{:S(2)}, u32[]{:S(2)}) %all-to-all-start.2) | async-done | bytes 4194336 | tf_op jit(solution)/shard_map/all_to_all | solution.py:113
  128.2 18.6 %shard_map.82 = bf16[512,1024]{1,0:T(8,128)(2,1)S(1)} custom-call(s32[16]{0:T(128)S(1)} %get-tuple-element.6.slots, s32[8]{0:T(128)S(1)} %fusion.16.live, bf16[512,1024]{1,0:T(8,128)(2,1)S(1)} %pad_maximum_fusion.q_ref, bf16[16,128,1024]{2,1,0:T(8,128)(2,1)} %bitcast.3.k0_ref.k1_ref, bf16[16,128,1024]{2,1,0:T(8,128)(2,1)} %bitcast.3.k0_ref.k1_ref, ...), custom_call_target="tpu_custom_call" | custom-call | flops 536870912 | bytes 10485760 | tf_op jit(solution)/shard_map/pallas_call | solution.py:59
  146.8 2.2 collective-permute-start.1
  149.0 0.1 slice.23
  149.1 0.9 collective-permute-done.1
  150.0 9.5 %convolution_convert_fusion = bf16[512,4096]{1,0:T(8,128)(2,1)} fusion(bf16[1024,4096]{1,0:T(8,128)(2,1)} %param.11, bf16[449,1024]{1,0:T(8,128)(2,1)S(1)} %slice.23, bf16[63,1024]{1,0:T(8,128)(2,1)S(1)} %collective-permute-done.1), kind=kOutput, calls=%fused_computation.7 | convolution fusion | flops 4299161600 | bytes 13631488 | tf_op jit(solution)/shard_map/dot_general | solution.py:124
  159.5 0.0 copy-start.2
  159.5 0.0 reduce-scatter.2.cloned.1.call-update
  159.6 80.1 %reduce-scatter.2.cloned.1.call-done = bf16[512,1024]{1,0:T(8,128)(2,1)} async-done(((bf16[512,4096]{1,0:T(8,128)(2,1)}), bf16[512,1024]{1,0:T(8,128)(2,1)}) %reduce-scatter.2.cloned.1.call-update) | async-done | bytes 1048592 | tf_op jit(solution)/shard_map/reduce_scatter | solution.py:125
  239.7 0.0 copy-done.2
  239.7 2.9 %convert_add_fusion = f32[512,1024]{1,0:T(8,128)} fusion(bf16[512,1024]{1,0:T(8,128)(2,1)} %reduce-scatter.2.cloned.1.call-done, bf16[512,1024]{1,0:T(8,128)(2,1)S(1)} %copy-done.2), kind=kLoop, calls=%fused_computation.11 | loop fusion | flops 1572864 | bytes 4194304 | tf_op jit(solution)/shard_map/add | solution.py:126
  (9 shorter events, 0.1 us)
Async XLA Ops:
  6.5 11.3 %copy-start = (bf16[8,128,1024]{2,1,0:T(8,128)(2,1)S(1)}, bf16[8,128,1024]{2,1,0:T(8,128)(2,1)}, u32[]{:S(2)}) copy-start(bf16[8,128,1024]{2,1,0:T(8,128)(2,1)} %param.12) | copy-start | bytes 6291460
  6.5 81.7 %all-gather.2.cloned.1.call-start = ((), (), s32[]{:S(2)}) async-start(), calls=%async_computation.4 | async-start | bytes 5242880 | tf_op jit(solution)/shard_map/all_gather | solution.py:84
  20.7 53.7 %all-to-all-start.1 = ((bf16[8,2,128,1024]{3,2,1,0:T(8,128)(2,1)}), bf16[8,2,128,1024]{3,2,1,0:T(8,128)(2,1)}, u32[]{:S(2)}, u32[]{:S(2)}) async-start(bf16[8,2,128,1024]{3,2,1,0:T(8,128)(2,1)} %bitcast.11), calls=%async_computation.1 | async-start | bytes 8388608 | tf_op jit(solution)/shard_map/all_to_all | solution.py:112
  74.3 17.1 %copy-start.3 = (f32[4096]{0:T(1024)S(1)}, f32[4096]{0:T(1024)}, u32[]{:S(2)}) copy-start(f32[4096]{0:T(1024)} %param.9) | copy-start | bytes 49156
  74.3 53.9 %all-to-all-start.2 = ((bf16[8,2,128,1024]{3,2,1,0:T(8,128)(2,1)}), bf16[8,2,128,1024]{3,2,1,0:T(8,128)(2,1)}, u32[]{:S(2)}, u32[]{:S(2)}) async-start(bf16[8,2,128,1024]{3,2,1,0:T(8,128)(2,1)} %bitcast.10), calls=%async_computation.2 | async-start | bytes 8388608 | tf_op jit(solution)/shard_map/all_to_all | solution.py:113
  79.1 160.6 %reduce-scatter.2.cloned.1.call-start = ((), (), s32[]{:S(2)}) async-start(), calls=%async_computation.5 | async-start | bytes 5242880 | tf_op jit(solution)/shard_map/reduce_scatter | solution.py:125
  88.2 3.4 %copy-start.1 = (bf16[512,4096]{1,0:T(8,128)(2,1)S(1)}, bf16[512,4096]{1,0:T(8,128)(2,1)}, u32[]{:S(2)}) copy-start(bf16[512,4096]{1,0:T(8,128)(2,1)} %all-gather.2.cloned.1.call-done) | copy-start | bytes 12582916
  98.9 3.2 %collective-permute-start = (bf16[63,1024]{1,0:T(8,128)(2,1)S(1)}, bf16[63,1024]{1,0:T(8,128)(2,1)S(1)}, u32[]{:S(2)}, u32[]{:S(2)}) collective-permute-start(bf16[63,1024]{1,0:T(8,128)(2,1)S(1)} %slice.21), channel_id=1, source_target_pairs={{4,0},{8,4},{12,8},{16,12},{20,16},{24,20},{28,24},{5,1},{9,5},{13... | collective-permute-start | bytes 387080 | tf_op jit(solution)/shard_map/ppermute | solution.py:22
  146.8 3.2 %collective-permute-start.1 = (bf16[63,1024]{1,0:T(8,128)(2,1)S(1)}, bf16[63,1024]{1,0:T(8,128)(2,1)S(1)}, u32[]{:S(2)}, u32[]{:S(2)}) collective-permute-start(bf16[63,1024]{1,0:T(8,128)(2,1)S(1)} %slice.22), channel_id=1, source_target_pairs={{0,4},{4,8},{8,12},{12,16},{16,20},{20,24},{24,28},{1,5},{5,9},{9,... | collective-permute-start | bytes 387080 | tf_op jit(solution)/shard_map/ppermute | solution.py:22
  159.5 80.2 %copy-start.2 = (bf16[512,1024]{1,0:T(8,128)(2,1)S(1)}, bf16[512,1024]{1,0:T(8,128)(2,1)}, u32[]{:S(2)}) copy-start(bf16[512,1024]{1,0:T(8,128)(2,1)} %param.8) | copy-start | bytes 3145732
Sparse Core Ops, SparseCore 0:
  8.9 79.2 all-gather.1
  159.7 79.9 reduce-scatter.1

commit v2 on v1

--- a/solution.py
+++ b/solution.py
@@ -72,6 +72,172 @@
             transcendentals=2 * rows * NBR * width // HS,
         ),
     )(slots, live, grouped, key_rows, key_rows, value_rows, value_rows)
+
+
+def project_kernel(
+    term_ref, w_ref, hidden_ref, out_ref, held, w_held, send_sem, recv_sem, w_sem
+):
+    me = lax.axis_index("mp")
+    count = lax.axis_size("mp")
+    width = hidden_ref.shape[1]
+    chunks = held.shape[2]
+    rows = held.shape[3]
+
+    def fetch(dest):
+        cols = pl.ds(pl.multiple_of(dest * width, width), width)
+        return pltpu.make_async_copy(w_ref.at[:, cols], w_held.at[dest], w_sem.at[dest])
+
+    for turn in range(count):
+        fetch(count - 1 - turn // 2 if turn % 2 == 0 else turn // 2).start()
+
+    barrier = pltpu.get_barrier_semaphore()
+
+    @pl.when(me > 0)
+    def _():
+        pl.semaphore_signal(
+            barrier, inc=1, device_id={"mp": me - 1}, device_id_type=pl.DeviceIdType.MESH
+        )
+
+    @pl.when(me < count - 1)
+    def _():
+        pl.semaphore_signal(
+            barrier, inc=1, device_id={"mp": me + 1}, device_id_type=pl.DeviceIdType.MESH
+        )
+
+    has_both = jnp.logical_and(me > 0, me < count - 1)
+
+    @pl.when(has_both)
+    def _():
+        pl.semaphore_wait(barrier, 2)
+
+    @pl.when(jnp.logical_not(has_both))
+    def _():
+        pl.semaphore_wait(barrier, 1)
+
+    def copy(way, turn, chunk, peer):
+        return pltpu.make_async_remote_copy(
+            src_ref=held.at[way, turn, chunk],
+            dst_ref=held.at[way, turn, chunk],
+            send_sem=send_sem.at[way, turn, chunk],
+            recv_sem=recv_sem.at[way, turn, chunk],
+            device_id={"mp": peer},
+            device_id_type=pl.DeviceIdType.MESH,
+        )
+
+    def own(chunk, dest):
+        first = pl.multiple_of(chunk * rows, rows)
+        return jnp.dot(
+            term_ref[pl.ds(first, rows), :], w_held[dest], preferred_element_type=jnp.float32
+        )
+
+    def pass_on(way, turn, chunk, dest, behind, ahead, has_behind):
+        @pl.when(chunk == 0)
+        def _():
+            fetch(dest).wait()
+
+        part = own(chunk, dest)
+
+        @pl.when(has_behind)
+        def _():
+            copy(way, turn, chunk, behind).wait_recv()
+            held[way, turn, chunk] = (
+                part + held[way, turn, chunk].astype(jnp.float32)
+            ).astype(jnp.bfloat16)
+
+        @pl.when(jnp.logical_not(has_behind))
+        def _():
+            held[way, turn, chunk] = part.astype(jnp.bfloat16)
+
+        copy(way, turn, chunk, ahead).start()
+
+    def step(index, carry):
+        turn = index // chunks
+        chunk = index % chunks
+        up = count - 1 - turn
+        down = turn
+
+        @pl.when(up > me)
+        def _():
+            pass_on(0, turn, chunk, up, me - 1, me + 1, me > 0)
+
+        @pl.when(down < me)
+        def _():
+            pass_on(1, turn, chunk, down, me + 1, me - 1, me < count - 1)
+
+        return carry
+
+    lax.fori_loop(0, (count - 1) * chunks, step, 0)
+    fetch(me).wait()
+
+    def finish_own(chunk, carry):
+        here = pl.ds(pl.multiple_of(chunk * rows, rows), rows)
+        out_ref[here, :] = own(chunk, me) + hidden_ref[here, :].astype(jnp.float32)
+        return carry
+
+    lax.fori_loop(0, chunks, finish_own, 0)
+
+    def finish(chunk, carry):
+        here = pl.ds(pl.multiple_of(chunk * rows, rows), rows)
+
+        @pl.when(me > 0)
+        def _():
+            copy(0, count - 1 - me, chunk, me - 1).wait_recv()
+            out_ref[here, :] += held[0, count - 1 - me, chunk].astype(jnp.float32)
+
+        @pl.when(me < count - 1)
+        def _():
+            copy(1, me, chunk, me + 1).wait_recv()
+            out_ref[here, :] += held[1, me, chunk].astype(jnp.float32)
+
+        return carry
+
+    lax.fori_loop(0, chunks, finish, 0)
+
+    def sent(index, carry):
+        turn = index // chunks
+        chunk = index % chunks
+
+        @pl.when(count - 1 - turn > me)
+        def _():
+            copy(0, turn, chunk, me + 1).wait_send()
+
+        @pl.when(turn < me)
+        def _():
+            copy(1, turn, chunk, me - 1).wait_send()
+
+        return carry
+
+    lax.fori_loop(0, (count - 1) * chunks, sent, 0)
+
+
+def project(terms, w_out, hidden):
+    tokens, width = hidden.shape
+    inner = terms.shape[1]
+    count = lax.axis_size("mp")
+    chunks = 4
+    rows = tokens // chunks
+    vmem = pl.BlockSpec(memory_space=pltpu.VMEM)
+    return pl.pallas_call(
+        project_kernel,
+        out_shape=jax.ShapeDtypeStruct((tokens, width), jnp.float32),
+        in_specs=[vmem, pl.BlockSpec(memory_space=pl.ANY), vmem],
+        out_specs=vmem,
+        scratch_shapes=[
+            pltpu.VMEM((2, count - 1, chunks, rows, width), jnp.bfloat16),
+            pltpu.VMEM((count, inner, width), jnp.bfloat16),
+            pltpu.SemaphoreType.DMA((2, count - 1, chunks)),
+            pltpu.SemaphoreType.DMA((2, count - 1, chunks)),
+            pltpu.SemaphoreType.DMA((count,)),
+        ],
+        compiler_params=pltpu.CompilerParams(
+            collective_id=0, has_side_effects=True, vmem_limit_bytes=32 * 2**20
+        ),
+        cost_estimate=pl.CostEstimate(
+            flops=2 * tokens * inner * width * count,
+            bytes_accessed=2 * inner * width * count + 8 * tokens * width,
+            transcendentals=0,
+        ),
+    )(terms, w_out, hidden)
 
 
 def shards(hidden, norm_gain, w_query, w_out, nb_keys, nb_values, neighbours, valid_spans):
@@ -121,9 +287,7 @@
     )
     previous = shifted(merged[tok_rows - SPAN + 1 :], "dp", 1)
     placed = jnp.concatenate([previous, merged[: tok_rows - SPAN + 1]], axis=0)
-    head_terms = jnp.dot(placed, w_out, preferred_element_type=jnp.float32).astype(jnp.bfloat16)
-    summed = lax.psum_scatter(head_terms, "mp", scatter_dimension=1, tiled=True)
-    return hidden.astype(jnp.float32) + summed.astype(jnp.float32)
+    return project(placed, w_out, hidden)
 
 
 def solution(mesh):

time: 252 us -> 251 us (level)
  Pallas kernels: 18.6 us -> 107 us
  waiting for transfers between devices: 163 us -> 83.2 us
  matrix products: 16.7 us -> 7.17 us
  local copies, waits for them, and re-layouts: 8.37 us -> 13 us
  other arithmetic: 7.36 us -> 4.67 us
    pallas_call x0 -> x1, Pallas kernels: none -> 88.2 us  [project(): pl.pallas_call(project_kernel, out_shape=jax.ShapeDtypeStruct((tokens, wi...]
    reduce_scatter x1 -> x0, waiting for transfers between devices: 80.1 us -> none  [shards(): summed = lax.psum_scatter(head_terms, 'mp', scatter_dimension=1, tiled=True)]
    dot_general x1 -> x0, matrix products: 9.53 us -> none  [shards(): jnp.dot(placed, w_out, preferred_element_type=jnp.float32)]
    unnamed x8 -> x11, local copies, waits for them, and re-layouts: 0.21 us -> 4.91 us
    add x1 -> x0, other arithmetic: 2.93 us -> none  [shards(): return hidden.astype(jnp.float32) + summed.astype(jnp.float32)]
  transfers between devices with their start and end apart: 6 -> 5, of which waited for: 6 -> 5; matrix products, arithmetic and copies ran while one was open for 8% -> 8% of each run, Pallas kernels for 0% -> 0%
where the time goes in v2:
time: 251 us; the launch traced here: 250 us
  Pallas kernels  107 us (43%)
  waiting for transfers between devices  83.2 us (33%)
  between operations  14.2 us (6%)
  local copies, waits for them, and re-layouts  13 us (5%)
  starting transfers between devices  12.9 us (5%)
  blocking collectives  8.18 us (3%)
  matrix products  7.17 us (3%)
  other arithmetic  4.67 us (2%)
    pallas_call x1, Pallas kernels, project(): pl.pallas_call(project_kernel, out_shape=jax.ShapeDtypeStruct((tokens, wi...  88.2 us
    all_to_all x1, waiting for transfers between devices, shards(): lax.all_to_all(nb_keys[safe_ids], 'dp', split_axis=0, concat_axis=0, tile...  44.8 us
    all_to_all x1, waiting for transfers between devices, shards(): lax.all_to_all(nb_values[safe_ids], 'dp', split_axis=0, concat_axis=0, ti...  26 us
    pallas_call x1, Pallas kernels, attention(): pl.pallas_call(attention_kernel, grid_spec=pltpu.PrefetchScalarGridSpec(n...  18.6 us
    all_gather x1, waiting for transfers between devices, shards(): lax.all_gather(hidden, 'mp', axis=1, tiled=True).astype(jnp.float32)  9.15 us
    all_to_all x1, blocking collectives, shards(): lax.all_to_all(request_table, 'dp', split_axis=0, concat_axis=0, tiled=True)  8.18 us
    dot_general x1, matrix products, shards(): jnp.dot(normed, w_query, preferred_element_type=jnp.float32)  7.17 us
  transfers between devices with their start and end apart: 5, of which 5 were waited for; matrix products, arithmetic and copies ran while one was open for 8% of the time, Pallas kernels for 0%

profile of v2, /device:TPU:8, one launch (start us, length us, event | category | flops | bytes accessed | tf_op | source)
XLA Modules:
  0.0 250.2 jit_solution(7066128493917382814)
XLA Ops:
  6.5 0.0 copy-start
  6.5 0.0 all-gather.2.cloned.1.call-start
  6.5 0.7 all-gather.2.cloned.1.call-update
  7.3 0.7 and_select_fusion
  7.9 0.1 copy.16
  8.0 0.1 reshape.73
  8.8 0.1 broadcast_in_dim.30
  8.9 0.1 and.24
  8.9 0.1 copy.17
  9.0 0.1 broadcast_in_dim.32
  9.1 0.2 convert_reduce_fusion
  9.3 0.1 fusion.10
  9.4 0.1 select_reduce_fusion
  9.5 0.1 select_n.45
  9.6 8.2 %all_to_all.16 = s32[8,1,2]{2,1,0:T(1,128)S(1)} all-to-all(s32[8,1,2]{2,1,0:T(1,128)S(1)} %bitcast.11), channel_id=1, replica_groups=mesh['dp'=8,'mp'=4] {'dp'}, dimensions={0} | all-to-all | bytes 128 | tf_op jit(solution)/shard_map/all_to_all | solution.py:276
  17.8 0.1 reshape.78
  17.9 0.0 copy-done
  17.9 2.8 %gather_fusion = bf16[16,128,1024]{2,1,0:T(8,128)(2,1)} fusion(bf16[8,128,1024]{2,1,0:T(8,128)(2,1)S(1)} %copy-done, s32[1024]{0:T(1024)S(1)} %pad_clamp_fusion), kind=kCustom, calls=%fused_computation | custom fusion | bytes 8388672 | tf_op jit(solution)/shard_map/gather | solution.py:278
  20.6 4.5 %all-to-all-start.1 = ((bf16[8,2,128,1024]{3,2,1,0:T(8,128)(2,1)}), bf16[8,2,128,1024]{3,2,1,0:T(8,128)(2,1)}, u32[]{:S(2)}, u32[]{:S(2)}) async-start(bf16[8,2,128,1024]{3,2,1,0:T(8,128)(2,1)} %bitcast.10), calls=%async_computation.1 | async-start | bytes 8388608 | tf_op jit(solution)/shard_map/all_to_all | solution.py:278
  25.2 4.4 %gather_fusion.1 = bf16[16,128,1024]{2,1,0:T(8,128)(2,1)} fusion(bf16[8,128,1024]{2,1,0:T(8,128)(2,1)} %param.13, s32[1024]{0:T(1024)S(1)} %pad_clamp_fusion), kind=kCustom, calls=%fused_computation.1 | custom fusion | bytes 8388672 | tf_op jit(solution)/shard_map/gather | solution.py:279
  29.6 44.8 %all-to-all-done.1 = bf16[8,2,128,1024]{3,2,1,0:T(8,128)(2,1)} async-done(((bf16[8,2,128,1024]{3,2,1,0:T(8,128)(2,1)}), bf16[8,2,128,1024]{3,2,1,0:T(8,128)(2,1)}, u32[]{:S(2)}, u32[]{:S(2)}) %all-to-all-start.1) | async-done | bytes 4194336 | tf_op jit(solution)/shard_map/all_to_all | solution.py:278
  74.3 0.0 copy-start.4
  74.3 4.7 %all-to-all-start.2 = ((bf16[8,2,128,1024]{3,2,1,0:T(8,128)(2,1)}), bf16[8,2,128,1024]{3,2,1,0:T(8,128)(2,1)}, u32[]{:S(2)}, u32[]{:S(2)}) async-start(bf16[8,2,128,1024]{3,2,1,0:T(8,128)(2,1)} %bitcast.9), calls=%async_computation.2 | async-start | bytes 8388608 | tf_op jit(solution)/shard_map/all_to_all | solution.py:279
  79.1 9.1 %all-gather.2.cloned.1.call-done = bf16[512,4096]{1,0:T(8,128)(2,1)} async-done(((bf16[512,1024]{1,0:T(8,128)(2,1)}), bf16[512,4096]{1,0:T(8,128)(2,1)}) %all-gather.2.cloned.1.call-update) | async-done | bytes 4194320 | tf_op jit(solution)/shard_map/all_gather | solution.py:250
  88.2 0.0 copy-start.3
  88.2 3.2 %fusion = f32[512]{0:T(512)S(1)} fusion(bf16[512,4096]{1,0:T(8,128)(2,1)} %all-gather.2.cloned.1.call-done), kind=kLoop, calls=%fused_computation.4 | loop fusion | flops 6290944 | bytes 4196352 | tf_op jit(solution)/shard_map/reduce_sum | solution.py:252
  91.4 0.0 copy-done.4
  91.5 0.2 copy-done.3
  91.7 7.2 %fusion.7 = bf16[512,1024]{1,0:T(8,128)(2,1)S(1)} fusion(bf16[4096,1024]{1,0:T(8,128)(2,1)} %param.10, bf16[512,4096]{1,0:T(8,128)(2,1)S(1)} %copy-done.3, f32[4096]{0:T(1024)S(1)} %copy-done.4, f32[512]{0:T(512)S(1)} %add_rsqrt_fusion), kind=kOutput, calls=%fused_computation.10 | convolution fusion | flops 4303880192 | bytes 13649920 | tf_op jit(solution)/shard_map/dot_general | solution.py:254
  98.9 1.3 collective-permute-start
  100.2 0.2 slice.20
  100.4 1.7 collective-permute-done
  102.1 0.1 pad_maximum_fusion.q_ref
  102.2 26.0 %all-to-all-done.2 = bf16[8,2,128,1024]{3,2,1,0:T(8,128)(2,1)} async-done(((bf16[8,2,128,1024]{3,2,1,0:T(8,128)(2,1)}), bf16[8,2,128,1024]{3,2,1,0:T(8,128)(2,1)}, u32[]{:S(2)}, u32[]{:S(2)}) %all-to-all-start.2) | async-done | bytes 4194336 | tf_op jit(solution)/shard_map/all_to_all | solution.py:279
  128.2 18.6 %shard_map.82 = bf16[512,1024]{1,0:T(8,128)(2,1)S(1)} custom-call(s32[16]{0:T(128)S(1)} %get-tuple-element.6.slots, s32[8]{0:T(128)S(1)} %fusion.12.live, bf16[512,1024]{1,0:T(8,128)(2,1)S(1)} %pad_maximum_fusion.q_ref, bf16[16,128,1024]{2,1,0:T(8,128)(2,1)} %bitcast.3.k0_ref.k1_ref, bf16[16,128,1024]{2,1,0:T(8,128)(2,1)} %bitcast.3.k0_ref.k1_ref, ...), custom_call_target="tpu_custom_call" | custom-call | flops 536870912 | bytes 10485760 | tf_op jit(solution)/shard_map/pallas_call | solution.py:59
  146.8 0.0 copy-start.1
  146.8 2.4 collective-permute-start.1
  149.2 0.1 slice.23
  149.2 0.9 collective-permute-done.1
  150.1 0.2 pad_maximum_fusion.1.term_ref
  150.4 0.0 copy-done.1
  150.4 0.0 copy-start.2
  150.4 3.4 %copy-done.2 = bf16[1024,4096]{1,0:T(8,128)(2,1)S(1)} copy-done((bf16[1024,4096]{1,0:T(8,128)(2,1)S(1)}, bf16[1024,4096]{1,0:T(8,128)(2,1)}, u32[]{:S(2)}) %copy-start.2) | copy-done | bytes 8388632
  153.8 88.2 %shard_map.83 = f32[512,1024]{1,0:T(8,128)S(1)} custom-call(bf16[512,1024]{1,0:T(8,128)(2,1)S(1)} %pad_maximum_fusion.1.term_ref, bf16[1024,4096]{1,0:T(8,128)(2,1)S(1)} %copy-done.2, bf16[512,1024]{1,0:T(8,128)(2,1)S(1)} %copy-done.1), custom_call_target="tpu_custom_call" | custom-call | flops 4294967296 | bytes 12582912 | tf_op jit(solution)/shard_map/pallas_call | solution.py:220
  242.0 1.3 copy.21
  (9 shorter events, 0.1 us)
Async XLA Ops:
  6.5 11.3 %copy-start = (bf16[8,128,1024]{2,1,0:T(8,128)(2,1)S(1)}, bf16[8,128,1024]{2,1,0:T(8,128)(2,1)}, u32[]{:S(2)}) copy-start(bf16[8,128,1024]{2,1,0:T(8,128)(2,1)} %param.12) | copy-start | bytes 6291460
  6.5 81.7 %all-gather.2.cloned.1.call-start = ((), (), s32[]{:S(2)}) async-start(), calls=%async_computation.3 | async-start | bytes 5242880 | tf_op jit(solution)/shard_map/all_gather | solution.py:250
  20.6 53.7 %all-to-all-start.1 = ((bf16[8,2,128,1024]{3,2,1,0:T(8,128)(2,1)}), bf16[8,2,128,1024]{3,2,1,0:T(8,128)(2,1)}, u32[]{:S(2)}, u32[]{:S(2)}) async-start(bf16[8,2,128,1024]{3,2,1,0:T(8,128)(2,1)} %bitcast.10), calls=%async_computation.1 | async-start | bytes 8388608 | tf_op jit(solution)/shard_map/all_to_all | solution.py:278
  74.3 17.1 %copy-start.4 = (f32[4096]{0:T(1024)S(1)}, f32[4096]{0:T(1024)}, u32[]{:S(2)}) copy-start(f32[4096]{0:T(1024)} %param.9) | copy-start | bytes 49156
  74.3 53.9 %all-to-all-start.2 = ((bf16[8,2,128,1024]{3,2,1,0:T(8,128)(2,1)}), bf16[8,2,128,1024]{3,2,1,0:T(8,128)(2,1)}, u32[]{:S(2)}, u32[]{:S(2)}) async-start(bf16[8,2,128,1024]{3,2,1,0:T(8,128)(2,1)} %bitcast.9), calls=%async_computation.2 | async-start | bytes 8388608 | tf_op jit(solution)/shard_map/all_to_all | solution.py:279
  88.2 3.4 %copy-start.3 = (bf16[512,4096]{1,0:T(8,128)(2,1)S(1)}, bf16[512,4096]{1,0:T(8,128)(2,1)}, u32[]{:S(2)}) copy-start(bf16[512,4096]{1,0:T(8,128)(2,1)} %all-gather.2.cloned.1.call-done) | copy-start | bytes 12582916
  98.9 3.2 %collective-permute-start = (bf16[63,1024]{1,0:T(8,128)(2,1)S(1)}, bf16[63,1024]{1,0:T(8,128)(2,1)S(1)}, u32[]{:S(2)}, u32[]{:S(2)}) collective-permute-start(bf16[63,1024]{1,0:T(8,128)(2,1)S(1)} %slice.21), channel_id=1, source_target_pairs={{4,0},{8,4},{12,8},{16,12},{20,16},{24,20},{28,24},{5,1},{9,5},{13... | collective-permute-start | bytes 387080 | tf_op jit(solution)/shard_map/ppermute | solution.py:22
  146.8 3.6 %copy-start.1 = (bf16[512,1024]{1,0:T(8,128)(2,1)S(1)}, bf16[512,1024]{1,0:T(8,128)(2,1)}, u32[]{:S(2)}) copy-start(bf16[512,1024]{1,0:T(8,128)(2,1)} %hidden_ref.1) | copy-start | bytes 3145732
  146.8 3.3 %collective-permute-start.1 = (bf16[63,1024]{1,0:T(8,128)(2,1)S(1)}, bf16[63,1024]{1,0:T(8,128)(2,1)S(1)}, u32[]{:S(2)}, u32[]{:S(2)}) collective-permute-start(bf16[63,1024]{1,0:T(8,128)(2,1)S(1)} %slice.22), channel_id=1, source_target_pairs={{0,4},{4,8},{8,12},{12,16},{16,20},{20,24},{24,28},{1,5},{5,9},{9,... | collective-permute-start | bytes 387080 | tf_op jit(solution)/shard_map/ppermute | solution.py:22
  150.4 3.4 %copy-start.2 = (bf16[1024,4096]{1,0:T(8,128)(2,1)S(1)}, bf16[1024,4096]{1,0:T(8,128)(2,1)}, u32[]{:S(2)}) copy-start(bf16[1024,4096]{1,0:T(8,128)(2,1)} %w_ref.1) | copy-start | bytes 25165828
Sparse Core Ops, SparseCore 0:
  8.9 79.2 all-gather.1

commit v3 on v2

--- a/solution.py
+++ b/solution.py
@@ -11,6 +11,7 @@
 HS = 128
 SPAN = 64
 NBR = 128
+DEPTH = 2
 
 
 eps = 1e-05
@@ -148,6 +149,12 @@
         def _():
             held[way, turn, chunk] = part.astype(jnp.bfloat16)
 
+        before = turn * chunks + chunk - DEPTH
+
+        @pl.when(before >= 0)
+        def _():
+            copy(way, before // chunks, before % chunks, ahead).wait_send()
+
         copy(way, turn, chunk, ahead).start()
 
     def step(index, carry):
@@ -196,12 +203,14 @@
     def sent(index, carry):
         turn = index // chunks
         chunk = index % chunks
-
-        @pl.when(count - 1 - turn > me)
+        ups = (count - 1 - me) * chunks
+        downs = me * chunks
+
+        @pl.when(jnp.logical_and(index < ups, index >= ups - DEPTH))
         def _():
             copy(0, turn, chunk, me + 1).wait_send()
 
-        @pl.when(turn < me)
+        @pl.when(jnp.logical_and(index < downs, index >= downs - DEPTH))
         def _():
             copy(1, turn, chunk, me - 1).wait_send()
 
@@ -230,7 +239,7 @@
             pltpu.SemaphoreType.DMA((count,)),
         ],
         compiler_params=pltpu.CompilerParams(
-            collective_id=0, has_side_effects=True, vmem_limit_bytes=32 * 2**20
+            collective_id=0, has_side_effects=True, vmem_limit_bytes=56 * 2**20
         ),
         cost_estimate=pl.CostEstimate(
             flops=2 * tokens * inner * width * count,
@@ -247,13 +256,13 @@
     inner_width = w_query.shape[1]
     peer_count = lax.axis_size("dp")
     most_slots = max(2, (2 * span_dev + peer_count - 1) // peer_count)
-    widened = lax.all_gather(hidden, "mp", axis=1, tiled=True).astype(jnp.float32)
+    following = shifted(hidden[: SPAN - 1], "dp", -1)
+    attending = jnp.concatenate([hidden[SPAN - 1 :], following], axis=0)
+    widened = lax.all_gather(attending, "mp", axis=1, tiled=True).astype(jnp.float32)
     normed = (
         widened * lax.rsqrt(jnp.mean(widened * widened, axis=1, keepdims=True) + eps) * norm_gain
     ).astype(jnp.bfloat16)
-    queries = jnp.dot(normed, w_query, preferred_element_type=jnp.float32).astype(jnp.bfloat16)
-    following = shifted(queries[: SPAN - 1], "dp", -1)
-    grouped = jnp.concatenate([queries[SPAN - 1 :], following], axis=0)
+    grouped = jnp.dot(normed, w_query, preferred_element_type=jnp.float32).astype(jnp.bfloat16)
     live_span = jnp.arange(span_dev, dtype=jnp.int32) < valid_spans[0]
     owners = (neighbours // stored).reshape(-1)
     slot_ids = (neighbours % stored).reshape(-1)

time: 251 us -> 261 us (1.040)
  Pallas kernels: 107 us -> 112 us
    pallas_call x1, Pallas kernels: 88.2 us -> 93.7 us  [project(): pl.pallas_call(project_kernel, out_shape=jax.ShapeDtypeStruct((tokens, wi...]
    all_to_all x1, waiting for transfers between devices: 26 us -> 29.4 us  [shards(): lax.all_to_all(nb_values[safe_ids], 'dp', split_axis=0, concat_axis=0, ti...]
  transfers between devices with their start and end apart: 5 -> 5, of which waited for: 5 -> 4; matrix products, arithmetic and copies ran while one was open for 8% -> 8% of each run, Pallas kernels for 0% -> 0%
where the time goes in v3:
time: 261 us; the launch traced here: 260 us
  Pallas kernels  112 us (43%)
  waiting for transfers between devices  84.1 us (32%)
  between operations  14.2 us (5%)
  local copies, waits for them, and re-layouts  13.8 us (5%)
  starting transfers between devices  11.9 us (5%)
  blocking collectives  9.59 us (4%)
  matrix products  7.17 us (3%)
  other arithmetic  6.65 us (3%)
    pallas_call x1, Pallas kernels, project(): pl.pallas_call(project_kernel, out_shape=jax.ShapeDtypeStruct((tokens, wi...  93.7 us
    all_to_all x1, waiting for transfers between devices, shards(): lax.all_to_all(nb_keys[safe_ids], 'dp', split_axis=0, concat_axis=0, tile...  44.7 us
    all_to_all x1, waiting for transfers between devices, shards(): lax.all_to_all(nb_values[safe_ids], 'dp', split_axis=0, concat_axis=0, ti...  29.4 us
    pallas_call x1, Pallas kernels, attention(): pl.pallas_call(attention_kernel, grid_spec=pltpu.PrefetchScalarGridSpec(n...  18.6 us
    all_to_all x1, blocking collectives, shards(): lax.all_to_all(request_table, 'dp', split_axis=0, concat_axis=0, tiled=True)  9.59 us
    all_gather x1, waiting for transfers between devices, shards(): lax.all_gather(attending, 'mp', axis=1, tiled=True).astype(jnp.float32)  9.12 us
    dot_general x1, matrix products, shards(): jnp.dot(normed, w_query, preferred_element_type=jnp.float32)  7.17 us
  transfers between devices with their start and end apart: 5, of which 4 were waited for; matrix products, arithmetic and copies ran while one was open for 8% of the time, Pallas kernels for 0%

profile of v3, /device:TPU:8, one launch (start us, length us, event | category | flops | bytes accessed | tf_op | source)
XLA Modules:
  0.0 259.6 jit_solution(1984141526277383553)
XLA Ops:
  6.5 0.0 copy-start
  6.5 0.0 all-gather.2.cloned.1.call-start
  6.5 1.1 slice.13
  7.6 1.3 collective-permute-start
  8.9 1.4 slice.12
  10.3 0.7 and_select_fusion
  11.0 0.1 copy.16
  11.1 0.1 reshape.73
  11.8 0.0 collective-permute-done
  11.9 1.1 pad_maximum_fusion
  12.9 0.0 all-gather.2.cloned.1.call-update
  13.0 0.1 broadcast_in_dim.30
  13.1 0.1 and.24
  13.1 0.1 copy.17
  13.2 0.1 broadcast_in_dim.32
  13.3 0.2 convert_reduce_fusion
  13.5 0.1 fusion.10
  13.6 0.1 select_reduce_fusion
  13.7 0.1 select_n.45
  13.8 9.6 %all_to_all.16 = s32[8,1,2]{2,1,0:T(1,128)S(1)} all-to-all(s32[8,1,2]{2,1,0:T(1,128)S(1)} %bitcast.11), channel_id=1, replica_groups=mesh['dp'=8,'mp'=4] {'dp'}, dimensions={0} | all-to-all | bytes 128 | tf_op jit(solution)/shard_map/all_to_all | solution.py:285
  23.4 0.1 reshape.78
  23.5 0.0 copy-done
  23.5 2.8 %gather_fusion = bf16[16,128,1024]{2,1,0:T(8,128)(2,1)} fusion(bf16[8,128,1024]{2,1,0:T(8,128)(2,1)S(1)} %copy-done, s32[1024]{0:T(1024)S(1)} %pad_clamp_fusion), kind=kCustom, calls=%fused_computation | custom fusion | bytes 8388672 | tf_op jit(solution)/shard_map/gather | solution.py:287
  26.3 4.5 %all-to-all-start.1 = ((bf16[8,2,128,1024]{3,2,1,0:T(8,128)(2,1)}), bf16[8,2,128,1024]{3,2,1,0:T(8,128)(2,1)}, u32[]{:S(2)}, u32[]{:S(2)}) async-start(bf16[8,2,128,1024]{3,2,1,0:T(8,128)(2,1)} %bitcast.10), calls=%async_computation.1 | async-start | bytes 8388608 | tf_op jit(solution)/shard_map/all_to_all | solution.py:287
  30.8 4.4 %gather_fusion.1 = bf16[16,128,1024]{2,1,0:T(8,128)(2,1)} fusion(bf16[8,128,1024]{2,1,0:T(8,128)(2,1)} %param.13, s32[1024]{0:T(1024)S(1)} %pad_clamp_fusion), kind=kCustom, calls=%fused_computation.1 | custom fusion | bytes 8388672 | tf_op jit(solution)/shard_map/gather | solution.py:288
  35.2 44.7 %all-to-all-done.1 = bf16[8,2,128,1024]{3,2,1,0:T(8,128)(2,1)} async-done(((bf16[8,2,128,1024]{3,2,1,0:T(8,128)(2,1)}), bf16[8,2,128,1024]{3,2,1,0:T(8,128)(2,1)}, u32[]{:S(2)}, u32[]{:S(2)}) %all-to-all-start.1) | async-done | bytes 4194336 | tf_op jit(solution)/shard_map/all_to_all | solution.py:287
  80.0 0.0 copy-start.2
  80.0 4.7 %all-to-all-start.2 = ((bf16[8,2,128,1024]{3,2,1,0:T(8,128)(2,1)}), bf16[8,2,128,1024]{3,2,1,0:T(8,128)(2,1)}, u32[]{:S(2)}, u32[]{:S(2)}) async-start(bf16[8,2,128,1024]{3,2,1,0:T(8,128)(2,1)} %bitcast.9), calls=%async_computation.2 | async-start | bytes 8388608 | tf_op jit(solution)/shard_map/all_to_all | solution.py:288
  84.7 9.1 %all-gather.2.cloned.1.call-done = bf16[512,4096]{1,0:T(8,128)(2,1)} async-done(((bf16[512,1024]{1,0:T(8,128)(2,1)}), bf16[512,4096]{1,0:T(8,128)(2,1)}) %all-gather.2.cloned.1.call-update) | async-done | bytes 4194320 | tf_op jit(solution)/shard_map/all_gather | solution.py:261
  93.8 0.0 copy-start.1
  93.8 3.2 %fusion = f32[512]{0:T(512)S(1)} fusion(bf16[512,4096]{1,0:T(8,128)(2,1)} %all-gather.2.cloned.1.call-done), kind=kLoop, calls=%fused_computation.4 | loop fusion | flops 6290944 | bytes 4196352 | tf_op jit(solution)/shard_map/reduce_sum | solution.py:263
  97.1 0.0 copy-done.2
  97.1 0.2 copy-done.1
  97.3 7.2 %fusion.7.q_ref = bf16[512,1024]{1,0:T(8,128)(2,1)S(1)} fusion(bf16[4096,1024]{1,0:T(8,128)(2,1)} %param.10, bf16[512,4096]{1,0:T(8,128)(2,1)S(1)} %copy-done.1, f32[4096]{0:T(1024)S(1)} %copy-done.2, f32[512]{0:T(512)S(1)} %add_rsqrt_fusion), kind=kOutput, calls=%fused_computation.10 | convolution fusion | flops 4303880192 | bytes 13649920 | tf_op jit(solution)/shard_map/dot_general | solution.py:265
  104.5 29.4 %all-to-all-done.2 = bf16[8,2,128,1024]{3,2,1,0:T(8,128)(2,1)} async-done(((bf16[8,2,128,1024]{3,2,1,0:T(8,128)(2,1)}), bf16[8,2,128,1024]{3,2,1,0:T(8,128)(2,1)}, u32[]{:S(2)}, u32[]{:S(2)}) %all-to-all-start.2) | async-done | bytes 4194336 | tf_op jit(solution)/shard_map/all_to_all | solution.py:288
  133.8 18.6 %shard_map.82 = bf16[512,1024]{1,0:T(8,128)(2,1)S(1)} custom-call(s32[16]{0:T(128)S(1)} %get-tuple-element.6.slots, s32[8]{0:T(128)S(1)} %fusion.12.live, bf16[512,1024]{1,0:T(8,128)(2,1)S(1)} %fusion.7.q_ref, bf16[16,128,1024]{2,1,0:T(8,128)(2,1)} %bitcast.3.k0_ref.k1_ref, bf16[16,128,1024]{2,1,0:T(8,128)(2,1)} %bitcast.3.k0_ref.k1_ref, ...), custom_call_target="tpu_custom_call" | custom-call | flops 536870912 | bytes 10485760 | tf_op jit(solution)/shard_map/pallas_call | solution.py:60
  152.4 1.3 collective-permute-start.1
  153.7 0.1 slice.21
  153.8 0.9 collective-permute-done.1
  154.7 1.2 pad_maximum_fusion.1.term_ref
  155.9 93.7 %shard_map.83 = f32[512,1024]{1,0:T(8,128)} custom-call(bf16[512,1024]{1,0:T(8,128)(2,1)} %pad_maximum_fusion.1.term_ref, bf16[1024,4096]{1,0:T(8,128)(2,1)} %w_ref.1, bf16[512,1024]{1,0:T(8,128)(2,1)} %hidden_ref.1), custom_call_target="tpu_custom_call" | custom-call | flops 4294967296 | bytes 12582912 | tf_op jit(solution)/shard_map/pallas_call | solution.py:229
  249.6 3.2 %copy.21 = f32[512,1024]{1,0:T(8,128)} copy(f32[512,1024]{1,0:T(8,128)} %shard_map.83) | data formatting | bytes 4194304
  (8 shorter events, 0.1 us)
Async XLA Ops:
  6.5 16.9 %copy-start = (bf16[8,128,1024]{2,1,0:T(8,128)(2,1)S(1)}, bf16[8,128,1024]{2,1,0:T(8,128)(2,1)}, u32[]{:S(2)}) copy-start(bf16[8,128,1024]{2,1,0:T(8,128)(2,1)} %param.12) | copy-start | bytes 6291460
  6.5 87.3 %all-gather.2.cloned.1.call-start = ((), (), s32[]{:S(2)}) async-start(), calls=%async_computation.3 | async-start | bytes 5242880 | tf_op jit(solution)/shard_map/all_gather | solution.py:261
  7.6 4.2 %collective-permute-start = (bf16[63,1024]{1,0:T(8,128)(2,1)S(1)}, bf16[63,1024]{1,0:T(8,128)(2,1)S(1)}, u32[]{:S(2)}, u32[]{:S(2)}) collective-permute-start(bf16[63,1024]{1,0:T(8,128)(2,1)S(1)} %slice.13), channel_id=1, source_target_pairs={{4,0},{8,4},{12,8},{16,12},{20,16},{24,20},{28,24},{5,1},{9,5},{13... | collective-permute-start | bytes 387080 | tf_op jit(solution)/shard_map/ppermute | solution.py:23
  26.3 53.7 %all-to-all-start.1 = ((bf16[8,2,128,1024]{3,2,1,0:T(8,128)(2,1)}), bf16[8,2,128,1024]{3,2,1,0:T(8,128)(2,1)}, u32[]{:S(2)}, u32[]{:S(2)}) async-start(bf16[8,2,128,1024]{3,2,1,0:T(8,128)(2,1)} %bitcast.10), calls=%async_computation.1 | async-start | bytes 8388608 | tf_op jit(solution)/shard_map/all_to_all | solution.py:287
  80.0 17.1 %copy-start.2 = (f32[4096]{0:T(1024)S(1)}, f32[4096]{0:T(1024)}, u32[]{:S(2)}) copy-start(f32[4096]{0:T(1024)} %param.9) | copy-start | bytes 49156
  80.0 53.9 %all-to-all-start.2 = ((bf16[8,2,128,1024]{3,2,1,0:T(8,128)(2,1)}), bf16[8,2,128,1024]{3,2,1,0:T(8,128)(2,1)}, u32[]{:S(2)}, u32[]{:S(2)}) async-start(bf16[8,2,128,1024]{3,2,1,0:T(8,128)(2,1)} %bitcast.9), calls=%async_computation.2 | async-start | bytes 8388608 | tf_op jit(solution)/shard_map/all_to_all | solution.py:288
  93.8 3.4 %copy-start.1 = (bf16[512,4096]{1,0:T(8,128)(2,1)S(1)}, bf16[512,4096]{1,0:T(8,128)(2,1)}, u32[]{:S(2)}) copy-start(bf16[512,4096]{1,0:T(8,128)(2,1)} %all-gather.2.cloned.1.call-done) | copy-start | bytes 12582916
  152.4 2.3 collective-permute-start.1
Sparse Core Ops, SparseCore 0:
  13.1 80.6 all-gather.1

commit v4 on v3

--- a/solution.py
+++ b/solution.py
@@ -11,7 +11,7 @@
 HS = 128
 SPAN = 64
 NBR = 128
-DEPTH = 2
+DEPTH = 3
 
 
 eps = 1e-05
@@ -157,19 +157,21 @@
 
         copy(way, turn, chunk, ahead).start()
 
-    def step(index, carry):
-        turn = index // chunks
-        chunk = index % chunks
-        up = count - 1 - turn
-        down = turn
-
-        @pl.when(up > me)
-        def _():
-            pass_on(0, turn, chunk, up, me - 1, me + 1, me > 0)
-
-        @pl.when(down < me)
-        def _():
-            pass_on(1, turn, chunk, down, me + 1, me - 1, me < count - 1)
+    def step(tick, carry):
+        up_index = tick - me
+        down_index = tick - (count - 1 - me)
+
+        @pl.when(jnp.logical_and(up_index >= 0, up_index < (count - 1 - me) * chunks))
+        def _():
+            turn = up_index // chunks
+            pass_on(
+                0, turn, up_index % chunks, count - 1 - turn, me - 1, me + 1, me > 0
+            )
+
+        @pl.when(jnp.logical_and(down_index >= 0, down_index < me * chunks))
+        def _():
+            turn = down_index // chunks
+            pass_on(1, turn, down_index % chunks, turn, me + 1, me - 1, me < count - 1)
 
         return carry
 
@@ -256,13 +258,13 @@
     inner_width = w_query.shape[1]
     peer_count = lax.axis_size("dp")
     most_slots = max(2, (2 * span_dev + peer_count - 1) // peer_count)
-    following = shifted(hidden[: SPAN - 1], "dp", -1)
-    attending = jnp.concatenate([hidden[SPAN - 1 :], following], axis=0)
-    widened = lax.all_gather(attending, "mp", axis=1, tiled=True).astype(jnp.float32)
+    widened = lax.all_gather(hidden, "mp", axis=1, tiled=True).astype(jnp.float32)
     normed = (
         widened * lax.rsqrt(jnp.mean(widened * widened, axis=1, keepdims=True) + eps) * norm_gain
     ).astype(jnp.bfloat16)
-    grouped = jnp.dot(normed, w_query, preferred_element_type=jnp.float32).astype(jnp.bfloat16)
+    queries = jnp.dot(normed, w_query, preferred_element_type=jnp.float32).astype(jnp.bfloat16)
+    following = shifted(queries[: SPAN - 1], "dp", -1)
+    grouped = jnp.concatenate([queries[SPAN - 1 :], following], axis=0)
     live_span = jnp.arange(span_dev, dtype=jnp.int32) < valid_spans[0]
     owners = (neighbours // stored).reshape(-1)
     slot_ids = (neighbours % stored).reshape(-1)

time: 261 us -> 239 us (0.916)
  Pallas kernels: 112 us -> 93.2 us
    pallas_call x1, Pallas kernels: 93.7 us -> 74.6 us  [project(): pl.pallas_call(project_kernel, out_shape=jax.ShapeDtypeStruct((tokens, wi...]
    all_to_all x1, waiting for transfers between devices: 29.4 us -> 26 us  [shards(): lax.all_to_all(nb_values[safe_ids], 'dp', split_axis=0, concat_axis=0, ti...]
  transfers between devices with their start and end apart: 5 -> 5, of which waited for: 4 -> 5; matrix products, arithmetic and copies ran while one was open for 8% -> 8% of each run, Pallas kernels for 0% -> 0%
where the time goes in v4:
time: 239 us; the launch traced here: 236 us
  Pallas kernels  93.2 us (39%)
  waiting for transfers between devices  83.2 us (35%)
  between operations  14.2 us (6%)
  starting transfers between devices  12.8 us (5%)
  local copies, waits for them, and re-layouts  11.5 us (5%)
  blocking collectives  8.18 us (3%)
  matrix products  7.17 us (3%)
  other arithmetic  5.66 us (2%)
    pallas_call x1, Pallas kernels, project(): pl.pallas_call(project_kernel, out_shape=jax.ShapeDtypeStruct((tokens, wi...  74.6 us
    all_to_all x1, waiting for transfers between devices, shards(): lax.all_to_all(nb_keys[safe_ids], 'dp', split_axis=0, concat_axis=0, tile...  44.7 us
    all_to_all x1, waiting for transfers between devices, shards(): lax.all_to_all(nb_values[safe_ids], 'dp', split_axis=0, concat_axis=0, ti...  26 us
    pallas_call x1, Pallas kernels, attention(): pl.pallas_call(attention_kernel, grid_spec=pltpu.PrefetchScalarGridSpec(n...  18.6 us
    all_gather x1, waiting for transfers between devices, shards(): lax.all_gather(hidden, 'mp', axis=1, tiled=True).astype(jnp.float32)  9.12 us
    all_to_all x1, blocking collectives, shards(): lax.all_to_all(request_table, 'dp', split_axis=0, concat_axis=0, tiled=True)  8.18 us
    dot_general x1, matrix products, shards(): jnp.dot(normed, w_query, preferred_element_type=jnp.float32)  7.17 us
  transfers between devices with their start and end apart: 5, of which 5 were waited for; matrix products, arithmetic and copies ran while one was open for 8% of the time, Pallas kernels for 0%

profile of v4, /device:TPU:8, one launch (start us, length us, event | category | flops | bytes accessed | tf_op | source)
XLA Modules:
  0.0 235.9 jit_solution(17041814110260013996)
XLA Ops:
  6.5 0.0 copy-start
  6.5 0.0 all-gather.2.cloned.1.call-start
  6.5 0.7 all-gather.2.cloned.1.call-update
  7.3 0.7 and_select_fusion
  7.9 0.1 copy.16
  8.0 0.1 reshape.73
  8.8 0.1 broadcast_in_dim.30
  8.9 0.1 and.24
  8.9 0.1 copy.17
  9.0 0.1 broadcast_in_dim.32
  9.1 0.2 convert_reduce_fusion
  9.3 0.1 fusion.10
  9.4 0.1 select_reduce_fusion
  9.5 0.1 select_n.45
  9.6 8.2 %all_to_all.16 = s32[8,1,2]{2,1,0:T(1,128)S(1)} all-to-all(s32[8,1,2]{2,1,0:T(1,128)S(1)} %bitcast.11), channel_id=1, replica_groups=mesh['dp'=8,'mp'=4] {'dp'}, dimensions={0} | all-to-all | bytes 128 | tf_op jit(solution)/shard_map/all_to_all | solution.py:287
  17.8 0.1 reshape.78
  17.9 0.0 copy-done
  17.9 2.8 %gather_fusion = bf16[16,128,1024]{2,1,0:T(8,128)(2,1)} fusion(bf16[8,128,1024]{2,1,0:T(8,128)(2,1)S(1)} %copy-done, s32[1024]{0:T(1024)S(1)} %pad_clamp_fusion), kind=kCustom, calls=%fused_computation | custom fusion | bytes 8388672 | tf_op jit(solution)/shard_map/gather | solution.py:289
  20.7 4.5 %all-to-all-start.1 = ((bf16[8,2,128,1024]{3,2,1,0:T(8,128)(2,1)}), bf16[8,2,128,1024]{3,2,1,0:T(8,128)(2,1)}, u32[]{:S(2)}, u32[]{:S(2)}) async-start(bf16[8,2,128,1024]{3,2,1,0:T(8,128)(2,1)} %bitcast.10), calls=%async_computation.1 | async-start | bytes 8388608 | tf_op jit(solution)/shard_map/all_to_all | solution.py:289
  25.2 4.4 %gather_fusion.1 = bf16[16,128,1024]{2,1,0:T(8,128)(2,1)} fusion(bf16[8,128,1024]{2,1,0:T(8,128)(2,1)} %param.13, s32[1024]{0:T(1024)S(1)} %pad_clamp_fusion), kind=kCustom, calls=%fused_computation.1 | custom fusion | bytes 8388672 | tf_op jit(solution)/shard_map/gather | solution.py:290
  29.6 44.7 %all-to-all-done.1 = bf16[8,2,128,1024]{3,2,1,0:T(8,128)(2,1)} async-done(((bf16[8,2,128,1024]{3,2,1,0:T(8,128)(2,1)}), bf16[8,2,128,1024]{3,2,1,0:T(8,128)(2,1)}, u32[]{:S(2)}, u32[]{:S(2)}) %all-to-all-start.1) | async-done | bytes 4194336 | tf_op jit(solution)/shard_map/all_to_all | solution.py:289
  74.3 0.0 copy-start.2
  74.3 4.7 %all-to-all-start.2 = ((bf16[8,2,128,1024]{3,2,1,0:T(8,128)(2,1)}), bf16[8,2,128,1024]{3,2,1,0:T(8,128)(2,1)}, u32[]{:S(2)}, u32[]{:S(2)}) async-start(bf16[8,2,128,1024]{3,2,1,0:T(8,128)(2,1)} %bitcast.9), calls=%async_computation.2 | async-start | bytes 8388608 | tf_op jit(solution)/shard_map/all_to_all | solution.py:290
  79.1 9.1 %all-gather.2.cloned.1.call-done = bf16[512,4096]{1,0:T(8,128)(2,1)} async-done(((bf16[512,1024]{1,0:T(8,128)(2,1)}), bf16[512,4096]{1,0:T(8,128)(2,1)}) %all-gather.2.cloned.1.call-update) | async-done | bytes 4194320 | tf_op jit(solution)/shard_map/all_gather | solution.py:261
  88.2 0.0 copy-start.1
  88.2 3.2 %fusion = f32[512]{0:T(512)S(1)} fusion(bf16[512,4096]{1,0:T(8,128)(2,1)} %all-gather.2.cloned.1.call-done), kind=kLoop, calls=%fused_computation.4 | loop fusion | flops 6290944 | bytes 4196352 | tf_op jit(solution)/shard_map/reduce_sum | solution.py:263
  91.4 0.0 copy-done.2
  91.5 0.2 copy-done.1
  91.7 7.2 %fusion.7 = bf16[512,1024]{1,0:T(8,128)(2,1)S(1)} fusion(bf16[4096,1024]{1,0:T(8,128)(2,1)} %param.10, bf16[512,4096]{1,0:T(8,128)(2,1)S(1)} %copy-done.1, f32[4096]{0:T(1024)S(1)} %copy-done.2, f32[512]{0:T(512)S(1)} %add_rsqrt_fusion), kind=kOutput, calls=%fused_computation.10 | convolution fusion | flops 4303880192 | bytes 13649920 | tf_op jit(solution)/shard_map/dot_general | solution.py:265
  98.9 1.3 collective-permute-start
  100.2 0.2 slice.20
  100.4 1.7 collective-permute-done
  102.1 0.1 pad_maximum_fusion.q_ref
  102.2 26.0 %all-to-all-done.2 = bf16[8,2,128,1024]{3,2,1,0:T(8,128)(2,1)} async-done(((bf16[8,2,128,1024]{3,2,1,0:T(8,128)(2,1)}), bf16[8,2,128,1024]{3,2,1,0:T(8,128)(2,1)}, u32[]{:S(2)}, u32[]{:S(2)}) %all-to-all-start.2) | async-done | bytes 4194336 | tf_op jit(solution)/shard_map/all_to_all | solution.py:290
  128.2 18.6 %shard_map.82 = bf16[512,1024]{1,0:T(8,128)(2,1)S(1)} custom-call(s32[16]{0:T(128)S(1)} %get-tuple-element.6.slots, s32[8]{0:T(128)S(1)} %fusion.12.live, bf16[512,1024]{1,0:T(8,128)(2,1)S(1)} %pad_maximum_fusion.q_ref, bf16[16,128,1024]{2,1,0:T(8,128)(2,1)} %bitcast.3.k0_ref.k1_ref, bf16[16,128,1024]{2,1,0:T(8,128)(2,1)} %bitcast.3.k0_ref.k1_ref, ...), custom_call_target="tpu_custom_call" | custom-call | flops 536870912 | bytes 10485760 | tf_op jit(solution)/shard_map/pallas_call | solution.py:60
  146.8 2.2 collective-permute-start.1
  149.1 0.1 slice.23
  149.1 0.9 collective-permute-done.1
  150.0 1.2 pad_maximum_fusion.1.term_ref
  151.2 74.6 %shard_map.83 = f32[512,1024]{1,0:T(8,128)} custom-call(bf16[512,1024]{1,0:T(8,128)(2,1)} %pad_maximum_fusion.1.term_ref, bf16[1024,4096]{1,0:T(8,128)(2,1)} %w_ref.1, bf16[512,1024]{1,0:T(8,128)(2,1)} %hidden_ref.1), custom_call_target="tpu_custom_call" | custom-call | flops 4294967296 | bytes 12582912 | tf_op jit(solution)/shard_map/pallas_call | solution.py:231
  225.9 3.2 %copy.21 = f32[512,1024]{1,0:T(8,128)} copy(f32[512,1024]{1,0:T(8,128)} %shard_map.83) | data formatting | bytes 4194304
  (9 shorter events, 0.1 us)
Async XLA Ops:
  6.5 11.3 %copy-start = (bf16[8,128,1024]{2,1,0:T(8,128)(2,1)S(1)}, bf16[8,128,1024]{2,1,0:T(8,128)(2,1)}, u32[]{:S(2)}) copy-start(bf16[8,128,1024]{2,1,0:T(8,128)(2,1)} %param.12) | copy-start | bytes 6291460
  6.5 81.7 %all-gather.2.cloned.1.call-start = ((), (), s32[]{:S(2)}) async-start(), calls=%async_computation.3 | async-start | bytes 5242880 | tf_op jit(solution)/shard_map/all_gather | solution.py:261
  20.7 53.7 %all-to-all-start.1 = ((bf16[8,2,128,1024]{3,2,1,0:T(8,128)(2,1)}), bf16[8,2,128,1024]{3,2,1,0:T(8,128)(2,1)}, u32[]{:S(2)}, u32[]{:S(2)}) async-start(bf16[8,2,128,1024]{3,2,1,0:T(8,128)(2,1)} %bitcast.10), calls=%async_computation.1 | async-start | bytes 8388608 | tf_op jit(solution)/shard_map/all_to_all | solution.py:289
  74.3 17.1 %copy-start.2 = (f32[4096]{0:T(1024)S(1)}, f32[4096]{0:T(1024)}, u32[]{:S(2)}) copy-start(f32[4096]{0:T(1024)} %param.9) | copy-start | bytes 49156
  74.3 53.9 %all-to-all-start.2 = ((bf16[8,2,128,1024]{3,2,1,0:T(8,128)(2,1)}), bf16[8,2,128,1024]{3,2,1,0:T(8,128)(2,1)}, u32[]{:S(2)}, u32[]{:S(2)}) async-start(bf16[8,2,128,1024]{3,2,1,0:T(8,128)(2,1)} %bitcast.9), calls=%async_computation.2 | async-start | bytes 8388608 | tf_op jit(solution)/shard_map/all_to_all | solution.py:290
  88.2 3.4 %copy-start.1 = (bf16[512,4096]{1,0:T(8,128)(2,1)S(1)}, bf16[512,4096]{1,0:T(8,128)(2,1)}, u32[]{:S(2)}) copy-start(bf16[512,4096]{1,0:T(8,128)(2,1)} %all-gather.2.cloned.1.call-done) | copy-start | bytes 12582916
  98.9 3.2 %collective-permute-start = (bf16[63,1024]{1,0:T(8,128)(2,1)S(1)}, bf16[63,1024]{1,0:T(8,128)(2,1)S(1)}, u32[]{:S(2)}, u32[]{:S(2)}) collective-permute-start(bf16[63,1024]{1,0:T(8,128)(2,1)S(1)} %slice.21), channel_id=1, source_target_pairs={{4,0},{8,4},{12,8},{16,12},{20,16},{24,20},{28,24},{5,1},{9,5},{13... | collective-permute-start | bytes 387080 | tf_op jit(solution)/shard_map/ppermute | solution.py:23
  146.8 3.2 %collective-permute-start.1 = (bf16[63,1024]{1,0:T(8,128)(2,1)S(1)}, bf16[63,1024]{1,0:T(8,128)(2,1)S(1)}, u32[]{:S(2)}, u32[]{:S(2)}) collective-permute-start(bf16[63,1024]{1,0:T(8,128)(2,1)S(1)} %slice.22), channel_id=1, source_target_pairs={{0,4},{4,8},{8,12},{12,16},{16,20},{20,24},{24,28},{1,5},{5,9},{9,... | collective-permute-start | bytes 387080 | tf_op jit(solution)/shard_map/ppermute | solution.py:23
Sparse Core Ops, SparseCore 0:
  8.9 79.2 all-gather.1

commit v5 on v4

--- a/solution.py
+++ b/solution.py
@@ -73,6 +73,98 @@
             transcendentals=2 * rows * NBR * width // HS,
         ),
     )(slots, live, grouped, key_rows, key_rows, value_rows, value_rows)
+
+
+def weights_kernel(slots, q_ref, k0_ref, k1_ref, out_ref):
+    factor = 1.0 / math.sqrt(HS)
+    for head in range(q_ref.shape[1] // HS):
+        cols = slice(head * HS, (head + 1) * HS)
+        keys = jnp.concatenate([k0_ref[0, :, cols], k1_ref[0, :, cols]], axis=0)
+        scores = (
+            lax.dot_general(
+                q_ref[:, cols],
+                keys,
+                (((1,), (1,)), ((), ())),
+                preferred_element_type=jnp.float32,
+            )
+            * factor
+        )
+        weights = jnp.exp(scores - jnp.max(scores, axis=1, keepdims=True))
+        total = jnp.sum(weights, axis=1, keepdims=True)
+        place = slice(head * 2 * NBR, (head + 1) * 2 * NBR)
+        out_ref[:, place] = (weights * (1.0 / total)).astype(jnp.bfloat16)
+
+
+def values_kernel(slots, live, weights_ref, v0_ref, v1_ref, out_ref):
+    keep = live[pl.program_id(0)] > 0
+    for head in range(out_ref.shape[1] // HS):
+        cols = slice(head * HS, (head + 1) * HS)
+        values = jnp.concatenate([v0_ref[0, :, cols], v1_ref[0, :, cols]], axis=0)
+        place = slice(head * 2 * NBR, (head + 1) * 2 * NBR)
+        merged = jnp.dot(weights_ref[:, place], values, preferred_element_type=jnp.float32)
+        out_ref[:, cols] = jnp.where(keep, merged, 0.0).astype(jnp.bfloat16)
+
+
+def weigh(slots, queries, key_rows):
+    rows, width = queries.shape
+    spans = rows // SPAN
+    spread = width // HS * 2 * NBR
+
+    def block(which):
+        return pl.BlockSpec((1, NBR, width), lambda span, slots: (slots[2 * span + which], 0, 0))
+
+    return pl.pallas_call(
+        weights_kernel,
+        grid_spec=pltpu.PrefetchScalarGridSpec(
+            num_scalar_prefetch=1,
+            grid=(spans,),
+            in_specs=[
+                pl.BlockSpec((SPAN, width), lambda span, slots: (span, 0)),
+                block(0),
+                block(1),
+            ],
+            out_specs=pl.BlockSpec((SPAN, spread), lambda span, slots: (span, 0)),
+        ),
+        out_shape=jax.ShapeDtypeStruct((rows, spread), jnp.bfloat16),
+        compiler_params=pltpu.CompilerParams(vmem_limit_bytes=24 * 2**20),
+        cost_estimate=pl.CostEstimate(
+            flops=4 * rows * NBR * width,
+            bytes_accessed=2 * rows * width + 4 * spans * NBR * width + 2 * rows * spread,
+            transcendentals=rows * spread,
+        ),
+    )(slots, queries, key_rows, key_rows)
+
+
+def combine(slots, live, weights, value_rows):
+    rows, spread = weights.shape
+    spans = rows // SPAN
+    width = value_rows.shape[2]
+
+    def block(which):
+        return pl.BlockSpec(
+            (1, NBR, width), lambda span, slots, live: (slots[2 * span + which], 0, 0)
+        )
+
+    return pl.pallas_call(
+        values_kernel,
+        grid_spec=pltpu.PrefetchScalarGridSpec(
+            num_scalar_prefetch=2,
+            grid=(spans,),
+            in_specs=[
+                pl.BlockSpec((SPAN, spread), lambda span, slots, live: (span, 0)),
+                block(0),
+                block(1),
+            ],
+            out_specs=pl.BlockSpec((SPAN, width), lambda span, slots, live: (span, 0)),
+        ),
+        out_shape=jax.ShapeDtypeStruct((rows, width), jnp.bfloat16),
+        compiler_params=pltpu.CompilerParams(vmem_limit_bytes=24 * 2**20),
+        cost_estimate=pl.CostEstimate(
+            flops=4 * rows * NBR * width,
+            bytes_accessed=2 * rows * width + 4 * spans * NBR * width + 2 * rows * spread,
+            transcendentals=0,
+        ),
+    )(slots, live, weights, value_rows, value_rows)
 
 
 def project_kernel(
@@ -264,7 +356,8 @@
     ).astype(jnp.bfloat16)
     queries = jnp.dot(normed, w_query, preferred_element_type=jnp.float32).astype(jnp.bfloat16)
     following = shifted(queries[: SPAN - 1], "dp", -1)
-    grouped = jnp.concatenate([queries[SPAN - 1 :], following], axis=0)
+    inside = queries[SPAN - 1 : tok_rows - 1]
+    crossing = jnp.concatenate([queries[tok_rows - 1 :], following], axis=0)
     live_span = jnp.arange(span_dev, dtype=jnp.int32) < valid_spans[0]
     owners = (neighbours // stored).reshape(-1)
     slot_ids = (neighbours % stored).reshape(-1)
@@ -289,15 +382,16 @@
     keys_back = lax.all_to_all(nb_keys[safe_ids], "dp", split_axis=0, concat_axis=0, tiled=True)
     values_back = lax.all_to_all(nb_values[safe_ids], "dp", split_axis=0, concat_axis=0, tiled=True)
     flat_slots = (peer_count * most_slots, NBR, inner_width)
-    merged = attention(
-        owners * most_slots + slot_rank,
-        live_span.astype(jnp.int32),
-        grouped,
-        keys_back.reshape(flat_slots),
-        values_back.reshape(flat_slots),
-    )
-    previous = shifted(merged[tok_rows - SPAN + 1 :], "dp", 1)
-    placed = jnp.concatenate([previous, merged[: tok_rows - SPAN + 1]], axis=0)
+    key_rows = keys_back.reshape(flat_slots)
+    value_rows = values_back.reshape(flat_slots)
+    slots = owners * most_slots + slot_rank
+    live = live_span.astype(jnp.int32)
+    split = 2 * (span_dev - 1)
+    weights = weigh(slots[:split], inside, key_rows)
+    last = attention(slots[split:], live[span_dev - 1 :], crossing, key_rows, value_rows)
+    previous = shifted(last[1:], "dp", 1)
+    merged = combine(slots[:split], live[: span_dev - 1], weights, value_rows)
+    placed = jnp.concatenate([previous, merged, last[:1]], axis=0)
     return project(placed, w_out, hidden)
 
 

time: 239 us -> 236 us (0.987)
    all_to_all x1, waiting for transfers between devices: 44.7 us -> 26 us  [shards(): lax.all_to_all(nb_keys[safe_ids], 'dp', split_axis=0, concat_axis=0, tile...]
    all_to_all x1, waiting for transfers between devices: 26 us -> 44.7 us  [shards(): lax.all_to_all(nb_values[safe_ids], 'dp', split_axis=0, concat_axis=0, ti...]
    pallas_call x1, Pallas kernels: 18.6 us -> 4.41 us  [attention(): pl.pallas_call(attention_kernel, grid_spec=pltpu.PrefetchScalarGridSpec(n...]
    pallas_call x0 -> x2, Pallas kernels: none -> 12.4 us  [the longest x1 6.74 us: weigh(): pl.pallas_call(weights_kernel, grid_spec=pltpu.PrefetchScalarGridSpec(num...]
  transfers between devices with their start and end apart: 5 -> 5, of which waited for: 5 -> 4; matrix products, arithmetic and copies ran while one was open for 8% -> 9% of each run, Pallas kernels for 0% -> 5%
where the time goes in v5:
time: 236 us; the launch traced here: 234 us
  Pallas kernels  91.6 us (39%)
  waiting for transfers between devices  81.9 us (35%)
  between operations  14.2 us (6%)
  starting transfers between devices  12.7 us (5%)
  local copies, waits for them, and re-layouts  12.1 us (5%)
  blocking collectives  8.18 us (3%)
  matrix products  7.2 us (3%)
  other arithmetic  5.61 us (2%)
    pallas_call x1, Pallas kernels, project(): pl.pallas_call(project_kernel, out_shape=jax.ShapeDtypeStruct((tokens, wi...  74.8 us
    all_to_all x1, waiting for transfers between devices, shards(): lax.all_to_all(nb_values[safe_ids], 'dp', split_axis=0, concat_axis=0, ti...  44.7 us
    all_to_all x1, waiting for transfers between devices, shards(): lax.all_to_all(nb_keys[safe_ids], 'dp', split_axis=0, concat_axis=0, tile...  26 us
    all_gather x1, waiting for transfers between devices, shards(): lax.all_gather(hidden, 'mp', axis=1, tiled=True).astype(jnp.float32)  9.17 us
    all_to_all x1, blocking collectives, shards(): lax.all_to_all(request_table, 'dp', split_axis=0, concat_axis=0, tiled=True)  8.18 us
    dot_general x1, matrix products, shards(): jnp.dot(normed, w_query, preferred_element_type=jnp.float32)  7.2 us
    pallas_call x1, Pallas kernels, weigh(): pl.pallas_call(weights_kernel, grid_spec=pltpu.PrefetchScalarGridSpec(num...  6.74 us
    pallas_call x1, Pallas kernels, combine(): pl.pallas_call(values_kernel, grid_spec=pltpu.PrefetchScalarGridSpec(num_...  5.71 us
  transfers between devices with their start and end apart: 5, of which 4 were waited for; matrix products, arithmetic and copies ran while one was open for 9% of the time, Pallas kernels for 5%

profile of v5, /device:TPU:8, one launch (start us, length us, event | category | flops | bytes accessed | tf_op | source)
XLA Modules:
  0.0 233.5 jit_solution(14341839143436708005)
XLA Ops:
  6.5 0.0 copy-start
  6.5 0.0 all-gather.2.cloned.1.call-start
  6.5 0.7 all-gather.2.cloned.1.call-update
  7.9 0.1 broadcast_in_dim.30
  8.0 0.1 and.24
  8.1 0.7 and_select_fusion
  8.8 0.1 copy.17
  8.9 0.1 broadcast_in_dim.32
  8.9 0.1 copy.16
  9.0 0.1 reshape.73
  9.1 0.2 convert_reduce_fusion
  9.3 0.1 fusion.10
  9.4 0.1 select_reduce_fusion
  9.5 0.1 select_n.45
  9.6 8.2 %all_to_all.16 = s32[8,1,2]{2,1,0:T(1,128)S(1)} all-to-all(s32[8,1,2]{2,1,0:T(1,128)S(1)} %bitcast.16), channel_id=1, replica_groups=mesh['dp'=8,'mp'=4] {'dp'}, dimensions={0} | all-to-all | bytes 128 | tf_op jit(solution)/shard_map/all_to_all | solution.py:380
  17.8 0.1 reshape.78
  17.9 0.0 copy-done
  17.9 2.8 %gather_fusion.1 = bf16[16,128,1024]{2,1,0:T(8,128)(2,1)} fusion(bf16[8,128,1024]{2,1,0:T(8,128)(2,1)S(1)} %copy-done, s32[1024]{0:T(1024)S(1)} %pad_clamp_fusion), kind=kCustom, calls=%fused_computation.1 | custom fusion | bytes 8388672 | tf_op jit(solution)/shard_map/gather | solution.py:383
  20.6 4.5 %all-to-all-start.2 = ((bf16[8,2,128,1024]{3,2,1,0:T(8,128)(2,1)}), bf16[8,2,128,1024]{3,2,1,0:T(8,128)(2,1)}, u32[]{:S(2)}, u32[]{:S(2)}) async-start(bf16[8,2,128,1024]{3,2,1,0:T(8,128)(2,1)} %bitcast.15), calls=%async_computation.2 | async-start | bytes 8388608 | tf_op jit(solution)/shard_map/all_to_all | solution.py:383
  25.2 4.4 %gather_fusion = bf16[16,128,1024]{2,1,0:T(8,128)(2,1)} fusion(bf16[8,128,1024]{2,1,0:T(8,128)(2,1)} %param.12, s32[1024]{0:T(1024)S(1)} %pad_clamp_fusion), kind=kCustom, calls=%fused_computation | custom fusion | bytes 8388672 | tf_op jit(solution)/shard_map/gather | solution.py:382
  29.6 44.7 %all-to-all-done.2 = bf16[8,2,128,1024]{3,2,1,0:T(8,128)(2,1)} async-done(((bf16[8,2,128,1024]{3,2,1,0:T(8,128)(2,1)}), bf16[8,2,128,1024]{3,2,1,0:T(8,128)(2,1)}, u32[]{:S(2)}, u32[]{:S(2)}) %all-to-all-start.2) | async-done | bytes 4194336 | tf_op jit(solution)/shard_map/all_to_all | solution.py:383
  74.3 0.0 copy-start.2
  74.3 4.7 %all-to-all-start.1 = ((bf16[8,2,128,1024]{3,2,1,0:T(8,128)(2,1)}), bf16[8,2,128,1024]{3,2,1,0:T(8,128)(2,1)}, u32[]{:S(2)}, u32[]{:S(2)}) async-start(bf16[8,2,128,1024]{3,2,1,0:T(8,128)(2,1)} %bitcast.14), calls=%async_computation.1 | async-start | bytes 8388608 | tf_op jit(solution)/shard_map/all_to_all | solution.py:382
  79.0 9.2 %all-gather.2.cloned.1.call-done = bf16[512,4096]{1,0:T(8,128)(2,1)} async-done(((bf16[512,1024]{1,0:T(8,128)(2,1)}), bf16[512,4096]{1,0:T(8,128)(2,1)}) %all-gather.2.cloned.1.call-update) | async-done | bytes 4194320 | tf_op jit(solution)/shard_map/all_gather | solution.py:353
  88.2 0.0 copy-start.1
  88.2 3.2 %fusion = f32[512]{0:T(512)S(1)} fusion(bf16[512,4096]{1,0:T(8,128)(2,1)} %all-gather.2.cloned.1.call-done), kind=kLoop, calls=%fused_computation.4 | loop fusion | flops 6290944 | bytes 4196352 | tf_op jit(solution)/shard_map/reduce_sum | solution.py:355
  91.4 0.0 copy-done.2
  91.5 0.2 copy-done.1
  91.7 7.2 %fusion.7 = bf16[512,1024]{1,0:T(8,128)(2,1)S(1)} fusion(bf16[4096,1024]{1,0:T(8,128)(2,1)} %param.10, bf16[512,4096]{1,0:T(8,128)(2,1)S(1)} %copy-done.1, f32[4096]{0:T(1024)S(1)} %copy-done.2, f32[512]{0:T(512)S(1)} %add_rsqrt_fusion), kind=kOutput, calls=%fused_computation.10 | convolution fusion | flops 4303880192 | bytes 13649920 | tf_op jit(solution)/shard_map/dot_general | solution.py:357
  98.9 1.3 collective-permute-start
  100.2 0.6 slice.29.live
  100.8 0.1 slice.28.slots
  100.9 1.3 collective-permute-done
  102.2 26.0 %all-to-all-done.1 = bf16[8,2,128,1024]{3,2,1,0:T(8,128)(2,1)} async-done(((bf16[8,2,128,1024]{3,2,1,0:T(8,128)(2,1)}), bf16[8,2,128,1024]{3,2,1,0:T(8,128)(2,1)}, u32[]{:S(2)}, u32[]{:S(2)}) %all-to-all-start.1) | async-done | bytes 4194336 | tf_op jit(solution)/shard_map/all_to_all | solution.py:382
  128.2 4.4 %shard_map.82 = bf16[64,1024]{1,0:T(8,128)(2,1)S(1)} custom-call(s32[2]{0:T(128)S(1)} %slice.28.slots, s32[1]{0:T(128)} %slice.29.live, bf16[64,1024]{1,0:T(8,128)(2,1)S(1)} %pad_maximum_fusion.1.q_ref, bf16[16,128,1024]{2,1,0:T(8,128)(2,1)} %bitcast.3.k0_ref.k1_ref, bf16[16,128,1024]{2,1,0:T(8,128)(2,1)} %bitcast.3.k0_ref.k1_ref, ...), custom_call_target="tpu_custom_call" | custom-call | flops 67108864 | bytes 1310720 | tf_op jit(solution)/shard_map/pallas_call | solution.py:60
  132.6 2.2 collective-permute-start.1
  134.8 0.2 slice.44.q_ref
  135.0 6.7 %shard_map.83.weights_ref = bf16[448,2048]{1,0:T(8,128)(2,1)S(1)} custom-call(s32[14]{0:T(128)S(1)} %bitcast.11, bf16[448,1024]{1,0:T(8,128)(2,1)S(1)} %slice.44.q_ref, bf16[16,128,1024]{2,1,0:T(8,128)(2,1)} %bitcast.3.k0_ref.k1_ref, bf16[16,128,1024]{2,1,0:T(8,128)(2,1)} %bitcast.3.k0_ref.k1_ref), custom_call_target="tpu_custom_call" | custom-call | flops 234881024 | bytes 6422528 | tf_op jit(solution)/shard_map/pallas_call | solution.py:116
  141.8 5.7 %shard_map.84 = bf16[448,1024]{1,0:T(8,128)(2,1)S(1)} custom-call(s32[14]{0:T(128)S(1)} %bitcast.12, s32[7]{0:T(128)S(1)} %bitcast.13, bf16[448,2048]{1,0:T(8,128)(2,1)S(1)} %shard_map.83.weights_ref, bf16[16,128,1024]{2,1,0:T(8,128)(2,1)} %bitcast.5.v0_ref.v1_ref, bf16[16,128,1024]{2,1,0:T(8,128)(2,1)} %bitcast.5.v0_ref.v1_ref), custom_call_target="tpu_custom_call" | custom-call | flops 234881024 | bytes 6422528 | tf_op jit(solution)/shard_map/pallas_call | solution.py:148
  147.5 0.0 collective-permute-done.1
  147.5 1.2 pad_maximum_fusion.term_ref
  148.7 74.8 %shard_map.85 = f32[512,1024]{1,0:T(8,128)} custom-call(bf16[512,1024]{1,0:T(8,128)(2,1)} %pad_maximum_fusion.term_ref, bf16[1024,4096]{1,0:T(8,128)(2,1)} %w_ref.1, bf16[512,1024]{1,0:T(8,128)(2,1)} %hidden_ref.1), custom_call_target="tpu_custom_call" | custom-call | flops 4294967296 | bytes 12582912 | tf_op jit(solution)/shard_map/pallas_call | solution.py:323
  223.5 3.2 %copy.21 = f32[512,1024]{1,0:T(8,128)} copy(f32[512,1024]{1,0:T(8,128)} %shard_map.85) | data formatting | bytes 4194304
  (12 shorter events, 0.2 us)
Async XLA Ops:
  6.5 11.3 %copy-start = (bf16[8,128,1024]{2,1,0:T(8,128)(2,1)S(1)}, bf16[8,128,1024]{2,1,0:T(8,128)(2,1)}, u32[]{:S(2)}) copy-start(bf16[8,128,1024]{2,1,0:T(8,128)(2,1)} %param.13) | copy-start | bytes 6291460
  6.5 81.7 %all-gather.2.cloned.1.call-start = ((), (), s32[]{:S(2)}) async-start(), calls=%async_computation.3 | async-start | bytes 5242880 | tf_op jit(solution)/shard_map/all_gather | solution.py:353
  20.6 53.7 %all-to-all-start.2 = ((bf16[8,2,128,1024]{3,2,1,0:T(8,128)(2,1)}), bf16[8,2,128,1024]{3,2,1,0:T(8,128)(2,1)}, u32[]{:S(2)}, u32[]{:S(2)}) async-start(bf16[8,2,128,1024]{3,2,1,0:T(8,128)(2,1)} %bitcast.15), calls=%async_computation.2 | async-start | bytes 8388608 | tf_op jit(solution)/shard_map/all_to_all | solution.py:383
  74.3 17.1 %copy-start.2 = (f32[4096]{0:T(1024)S(1)}, f32[4096]{0:T(1024)}, u32[]{:S(2)}) copy-start(f32[4096]{0:T(1024)} %param.9) | copy-start | bytes 49156
  74.3 53.8 %all-to-all-start.1 = ((bf16[8,2,128,1024]{3,2,1,0:T(8,128)(2,1)}), bf16[8,2,128,1024]{3,2,1,0:T(8,128)(2,1)}, u32[]{:S(2)}, u32[]{:S(2)}) async-start(bf16[8,2,128,1024]{3,2,1,0:T(8,128)(2,1)} %bitcast.14), calls=%async_computation.1 | async-start | bytes 8388608 | tf_op jit(solution)/shard_map/all_to_all | solution.py:382
  88.2 3.4 %copy-start.1 = (bf16[512,4096]{1,0:T(8,128)(2,1)S(1)}, bf16[512,4096]{1,0:T(8,128)(2,1)}, u32[]{:S(2)}) copy-start(bf16[512,4096]{1,0:T(8,128)(2,1)} %all-gather.2.cloned.1.call-done) | copy-start | bytes 12582916
  98.9 3.2 %collective-permute-start = (bf16[63,1024]{1,0:T(8,128)(2,1)S(1)}, bf16[63,1024]{1,0:T(8,128)(2,1)S(1)}, u32[]{:S(2)}, u32[]{:S(2)}) collective-permute-start(bf16[63,1024]{1,0:T(8,128)(2,1)S(1)} %slice.42), channel_id=1, source_target_pairs={{4,0},{8,4},{12,8},{16,12},{20,16},{24,20},{28,24},{5,1},{9,5},{13... | collective-permute-start | bytes 387080 | tf_op jit(solution)/shard_map/ppermute | solution.py:23
  132.6 14.9 %collective-permute-start.1 = (bf16[63,1024]{1,0:T(8,128)(2,1)S(1)}, bf16[63,1024]{1,0:T(8,128)(2,1)S(1)}, u32[]{:S(2)}, u32[]{:S(2)}) collective-permute-start(bf16[63,1024]{1,0:T(8,128)(2,1)S(1)} %slice.43), channel_id=1, source_target_pairs={{0,4},{4,8},{8,12},{12,16},{16,20},{20,24},{24,28},{1,5},{5,9},{9,... | collective-permute-start | bytes 387080 | tf_op jit(solution)/shard_map/ppermute | solution.py:23
Sparse Core Ops, SparseCore 0:
  8.9 79.2 all-gather.1

commit v6 on v5

--- a/solution.py
+++ b/solution.py
@@ -355,9 +355,6 @@
         widened * lax.rsqrt(jnp.mean(widened * widened, axis=1, keepdims=True) + eps) * norm_gain
     ).astype(jnp.bfloat16)
     queries = jnp.dot(normed, w_query, preferred_element_type=jnp.float32).astype(jnp.bfloat16)
-    following = shifted(queries[: SPAN - 1], "dp", -1)
-    inside = queries[SPAN - 1 : tok_rows - 1]
-    crossing = jnp.concatenate([queries[tok_rows - 1 :], following], axis=0)
     live_span = jnp.arange(span_dev, dtype=jnp.int32) < valid_spans[0]
     owners = (neighbours // stored).reshape(-1)
     slot_ids = (neighbours % stored).reshape(-1)
@@ -380,14 +377,18 @@
         lax.all_to_all(request_table, "dp", split_axis=0, concat_axis=0, tiled=True), 0
     )
     keys_back = lax.all_to_all(nb_keys[safe_ids], "dp", split_axis=0, concat_axis=0, tiled=True)
-    values_back = lax.all_to_all(nb_values[safe_ids], "dp", split_axis=0, concat_axis=0, tiled=True)
+    wanted, keys_back = lax.optimization_barrier((nb_values[safe_ids], keys_back))
+    values_back = lax.all_to_all(wanted, "dp", split_axis=0, concat_axis=0, tiled=True)
     flat_slots = (peer_count * most_slots, NBR, inner_width)
     key_rows = keys_back.reshape(flat_slots)
     value_rows = values_back.reshape(flat_slots)
     slots = owners * most_slots + slot_rank
     live = live_span.astype(jnp.int32)
     split = 2 * (span_dev - 1)
-    weights = weigh(slots[:split], inside, key_rows)
+    weights = weigh(slots[:split], queries[SPAN - 1 : tok_rows - 1], key_rows)
+    edge, weights = lax.optimization_barrier((queries[: SPAN - 1], weights))
+    following = shifted(edge, "dp", -1)
+    crossing = jnp.concatenate([queries[tok_rows - 1 :], following], axis=0)
     last = attention(slots[split:], live[span_dev - 1 :], crossing, key_rows, value_rows)
     previous = shifted(last[1:], "dp", 1)
     merged = combine(slots[:split], live[: span_dev - 1], weights, value_rows)

time: 236 us -> 229 us (0.970)
  waiting for transfers between devices: 81.9 us -> 73.7 us
    all_to_all x1, waiting for transfers between devices: 44.7 us -> 17.7 us  [shards(): lax.all_to_all(wanted, 'dp', split_axis=0, concat_axis=0, tiled=True)]
    all_to_all x1, waiting for transfers between devices: 26 us -> 44.8 us  [shards(): lax.all_to_all(nb_keys[safe_ids], 'dp', split_axis=0, concat_axis=0, tile...]
where the time goes in v6:
time: 229 us; the launch traced here: 227 us
  Pallas kernels  91.7 us (40%)
  waiting for transfers between devices  73.7 us (32%)
  between operations  14.2 us (6%)
  local copies, waits for them, and re-layouts  13.3 us (6%)
  starting transfers between devices  12.7 us (6%)
  blocking collectives  8.18 us (4%)
  matrix products  7.2 us (3%)
  other arithmetic  5.61 us (2%)
    pallas_call x1, Pallas kernels, project(): pl.pallas_call(project_kernel, out_shape=jax.ShapeDtypeStruct((tokens, wi...  74.8 us
    all_to_all x1, waiting for transfers between devices, shards(): lax.all_to_all(nb_keys[safe_ids], 'dp', split_axis=0, concat_axis=0, tile...  44.8 us
    all_to_all x1, waiting for transfers between devices, shards(): lax.all_to_all(wanted, 'dp', split_axis=0, concat_axis=0, tiled=True)  17.7 us
    all_gather x1, waiting for transfers between devices, shards(): lax.all_gather(hidden, 'mp', axis=1, tiled=True).astype(jnp.float32)  9.2 us
    all_to_all x1, blocking collectives, shards(): lax.all_to_all(request_table, 'dp', split_axis=0, concat_axis=0, tiled=True)  8.18 us
    dot_general x1, matrix products, shards(): jnp.dot(normed, w_query, preferred_element_type=jnp.float32)  7.2 us
    pallas_call x1, Pallas kernels, weigh(): pl.pallas_call(weights_kernel, grid_spec=pltpu.PrefetchScalarGridSpec(num...  6.73 us
    pallas_call x1, Pallas kernels, combine(): pl.pallas_call(values_kernel, grid_spec=pltpu.PrefetchScalarGridSpec(num_...  5.71 us
  transfers between devices with their start and end apart: 5, of which 4 were waited for; matrix products, arithmetic and copies ran while one was open for 9% of the time, Pallas kernels for 5%

profile of v6, /device:TPU:8, one launch (start us, length us, event | category | flops | bytes accessed | tf_op | source)
XLA Modules:
  0.0 226.6 jit_solution(14370967809713345458)
XLA Ops:
  6.5 0.0 copy-start
  6.5 0.0 all-gather.2.cloned.1.call-start
  6.5 0.7 all-gather.2.cloned.1.call-update
  7.9 0.1 broadcast_in_dim.30
  8.0 0.1 and.24
  8.1 0.7 and_select_fusion
  8.8 0.1 copy.17
  8.9 0.1 broadcast_in_dim.32
  8.9 0.1 copy.16
  9.0 0.1 reshape.73
  9.1 0.2 convert_reduce_fusion
  9.3 0.1 fusion.10
  9.4 0.1 select_reduce_fusion
  9.5 0.1 select_n.45
  9.6 8.2 %all_to_all.16 = s32[8,1,2]{2,1,0:T(1,128)S(1)} all-to-all(s32[8,1,2]{2,1,0:T(1,128)S(1)} %bitcast.16), channel_id=1, replica_groups=mesh['dp'=8,'mp'=4] {'dp'}, dimensions={0} | all-to-all | bytes 128 | tf_op jit(solution)/shard_map/all_to_all | solution.py:377
  17.8 0.1 reshape.78
  17.9 0.0 copy-done
  17.9 2.8 %gather_fusion.1 = bf16[16,128,1024]{2,1,0:T(8,128)(2,1)} fusion(bf16[8,128,1024]{2,1,0:T(8,128)(2,1)S(1)} %copy-done, s32[1024]{0:T(1024)S(1)} %pad_clamp_fusion), kind=kCustom, calls=%fused_computation.1 | custom fusion | bytes 8388672 | tf_op jit(solution)/shard_map/gather | solution.py:379
  20.6 4.5 %all-to-all-start.1 = ((bf16[8,2,128,1024]{3,2,1,0:T(8,128)(2,1)}), bf16[8,2,128,1024]{3,2,1,0:T(8,128)(2,1)}, u32[]{:S(2)}, u32[]{:S(2)}) async-start(bf16[8,2,128,1024]{3,2,1,0:T(8,128)(2,1)} %bitcast.15), calls=%async_computation.1 | async-start | bytes 8388608 | tf_op jit(solution)/shard_map/all_to_all | solution.py:379
  25.2 4.4 %gather_fusion = bf16[16,128,1024]{2,1,0:T(8,128)(2,1)} fusion(bf16[8,128,1024]{2,1,0:T(8,128)(2,1)} %param.13, s32[1024]{0:T(1024)S(1)} %pad_clamp_fusion), kind=kCustom, calls=%fused_computation | custom fusion | bytes 8388672 | tf_op jit(solution)/shard_map/gather | solution.py:380
  29.6 44.8 %all-to-all-done.1 = bf16[8,2,128,1024]{3,2,1,0:T(8,128)(2,1)} async-done(((bf16[8,2,128,1024]{3,2,1,0:T(8,128)(2,1)}), bf16[8,2,128,1024]{3,2,1,0:T(8,128)(2,1)}, u32[]{:S(2)}, u32[]{:S(2)}) %all-to-all-start.1) | async-done | bytes 4194336 | tf_op jit(solution)/shard_map/all_to_all | solution.py:379
  74.3 0.0 copy-start.4
  74.3 4.7 %all-to-all-start.2 = ((bf16[8,2,128,1024]{3,2,1,0:T(8,128)(2,1)}), bf16[8,2,128,1024]{3,2,1,0:T(8,128)(2,1)}, u32[]{:S(2)}, u32[]{:S(2)}) async-start(bf16[8,2,128,1024]{3,2,1,0:T(8,128)(2,1)} %bitcast.14), calls=%async_computation.2 | async-start | bytes 8388608 | tf_op jit(solution)/shard_map/all_to_all | solution.py:381
  79.0 9.2 %all-gather.2.cloned.1.call-done = bf16[512,4096]{1,0:T(8,128)(2,1)} async-done(((bf16[512,1024]{1,0:T(8,128)(2,1)}), bf16[512,4096]{1,0:T(8,128)(2,1)}) %all-gather.2.cloned.1.call-update) | async-done | bytes 4194320 | tf_op jit(solution)/shard_map/all_gather | solution.py:353
  88.2 0.0 copy-start.3
  88.2 3.2 %fusion = f32[512]{0:T(512)S(1)} fusion(bf16[512,4096]{1,0:T(8,128)(2,1)} %all-gather.2.cloned.1.call-done), kind=kLoop, calls=%fused_computation.4 | loop fusion | flops 6290944 | bytes 4196352 | tf_op jit(solution)/shard_map/reduce_sum | solution.py:355
  91.4 0.0 copy-done.4
  91.5 0.2 copy-done.3
  91.7 7.2 %fusion.7 = bf16[512,1024]{1,0:T(8,128)(2,1)S(1)} fusion(bf16[4096,1024]{1,0:T(8,128)(2,1)} %param.10, bf16[512,4096]{1,0:T(8,128)(2,1)S(1)} %copy-done.3, f32[4096]{0:T(1024)S(1)} %copy-done.4, f32[512]{0:T(512)S(1)} %add_rsqrt_fusion), kind=kOutput, calls=%fused_computation.10 | convolution fusion | flops 4303880192 | bytes 13649920 | tf_op jit(solution)/shard_map/dot_general | solution.py:357
  98.9 0.2 slice.43.q_ref
  99.1 6.7 %shard_map.82.weights_ref = bf16[448,2048]{1,0:T(8,128)(2,1)S(1)} custom-call(s32[14]{0:T(128)S(1)} %bitcast.11, bf16[448,1024]{1,0:T(8,128)(2,1)S(1)} %slice.43.q_ref, bf16[16,128,1024]{2,1,0:T(8,128)(2,1)} %bitcast.4.k0_ref.k1_ref, bf16[16,128,1024]{2,1,0:T(8,128)(2,1)} %bitcast.4.k0_ref.k1_ref), custom_call_target="tpu_custom_call" | custom-call | flops 234881024 | bytes 6422528 | tf_op jit(solution)/shard_map/pallas_call | solution.py:116
  105.9 0.0 copy-start.1
  105.9 1.2 copy-done.1
  107.1 1.3 collective-permute-start
  108.4 0.1 slice.28.slots
  108.5 0.6 slice.29.live
  109.1 1.3 collective-permute-done
  110.4 17.7 %all-to-all-done.2 = bf16[8,2,128,1024]{3,2,1,0:T(8,128)(2,1)} async-done(((bf16[8,2,128,1024]{3,2,1,0:T(8,128)(2,1)}), bf16[8,2,128,1024]{3,2,1,0:T(8,128)(2,1)}, u32[]{:S(2)}, u32[]{:S(2)}) %all-to-all-start.2) | async-done | bytes 4194336 | tf_op jit(solution)/shard_map/all_to_all | solution.py:381
  128.1 0.0 copy-start.2
  128.1 4.5 %shard_map.83 = bf16[64,1024]{1,0:T(8,128)(2,1)S(1)} custom-call(s32[2]{0:T(128)S(1)} %slice.28.slots, s32[1]{0:T(128)} %slice.29.live, bf16[64,1024]{1,0:T(8,128)(2,1)S(1)} %pad_maximum_fusion.1.q_ref, bf16[16,128,1024]{2,1,0:T(8,128)(2,1)} %bitcast.4.k0_ref.k1_ref, bf16[16,128,1024]{2,1,0:T(8,128)(2,1)} %bitcast.4.k0_ref.k1_ref, ...), custom_call_target="tpu_custom_call" | custom-call | flops 67108864 | bytes 1310720 | tf_op jit(solution)/shard_map/pallas_call | solution.py:60
  132.6 2.2 collective-permute-start.1
  134.8 0.0 copy-done.2
  134.8 5.7 %shard_map.84 = bf16[448,1024]{1,0:T(8,128)(2,1)S(1)} custom-call(s32[14]{0:T(128)S(1)} %bitcast.12, s32[7]{0:T(128)S(1)} %bitcast.13, bf16[448,2048]{1,0:T(8,128)(2,1)S(1)} %copy-done.2, bf16[16,128,1024]{2,1,0:T(8,128)(2,1)} %bitcast.5.v0_ref.v1_ref, bf16[16,128,1024]{2,1,0:T(8,128)(2,1)} %bitcast.5.v0_ref.v1_ref), custom_call_target="tpu_custom_call" | custom-call | flops 234881024 | bytes 6422528 | tf_op jit(solution)/shard_map/pallas_call | solution.py:148
  140.6 0.0 collective-permute-done.1
  140.6 1.2 pad_maximum_fusion.term_ref
  141.8 74.8 %shard_map.85 = f32[512,1024]{1,0:T(8,128)} custom-call(bf16[512,1024]{1,0:T(8,128)(2,1)} %pad_maximum_fusion.term_ref, bf16[1024,4096]{1,0:T(8,128)(2,1)} %w_ref.1, bf16[512,1024]{1,0:T(8,128)(2,1)} %hidden_ref.1), custom_call_target="tpu_custom_call" | custom-call | flops 4294967296 | bytes 12582912 | tf_op jit(solution)/shard_map/pallas_call | solution.py:323
  216.6 3.2 %copy.21 = f32[512,1024]{1,0:T(8,128)} copy(f32[512,1024]{1,0:T(8,128)} %shard_map.85) | data formatting | bytes 4194304
  (12 shorter events, 0.2 us)
Async XLA Ops:
  6.5 11.3 %copy-start = (bf16[8,128,1024]{2,1,0:T(8,128)(2,1)S(1)}, bf16[8,128,1024]{2,1,0:T(8,128)(2,1)}, u32[]{:S(2)}) copy-start(bf16[8,128,1024]{2,1,0:T(8,128)(2,1)} %param.12) | copy-start | bytes 6291460
  6.5 81.7 %all-gather.2.cloned.1.call-start = ((), (), s32[]{:S(2)}) async-start(), calls=%async_computation.3 | async-start | bytes 5242880 | tf_op jit(solution)/shard_map/all_gather | solution.py:353
  20.6 53.7 %all-to-all-start.1 = ((bf16[8,2,128,1024]{3,2,1,0:T(8,128)(2,1)}), bf16[8,2,128,1024]{3,2,1,0:T(8,128)(2,1)}, u32[]{:S(2)}, u32[]{:S(2)}) async-start(bf16[8,2,128,1024]{3,2,1,0:T(8,128)(2,1)} %bitcast.15), calls=%async_computation.1 | async-start | bytes 8388608 | tf_op jit(solution)/shard_map/all_to_all | solution.py:379
  74.3 17.1 %copy-start.4 = (f32[4096]{0:T(1024)S(1)}, f32[4096]{0:T(1024)}, u32[]{:S(2)}) copy-start(f32[4096]{0:T(1024)} %param.9) | copy-start | bytes 49156
  74.3 53.8 %all-to-all-start.2 = ((bf16[8,2,128,1024]{3,2,1,0:T(8,128)(2,1)}), bf16[8,2,128,1024]{3,2,1,0:T(8,128)(2,1)}, u32[]{:S(2)}, u32[]{:S(2)}) async-start(bf16[8,2,128,1024]{3,2,1,0:T(8,128)(2,1)} %bitcast.14), calls=%async_computation.2 | async-start | bytes 8388608 | tf_op jit(solution)/shard_map/all_to_all | solution.py:381
  88.2 3.4 %copy-start.3 = (bf16[512,4096]{1,0:T(8,128)(2,1)S(1)}, bf16[512,4096]{1,0:T(8,128)(2,1)}, u32[]{:S(2)}) copy-start(bf16[512,4096]{1,0:T(8,128)(2,1)} %all-gather.2.cloned.1.call-done) | copy-start | bytes 12582916
  105.9 1.2 copy-start.1
  107.1 3.2 %collective-permute-start = (bf16[63,1024]{1,0:T(8,128)(2,1)S(1)}, bf16[63,1024]{1,0:T(8,128)(2,1)S(1)}, u32[]{:S(2)}, u32[]{:S(2)}) collective-permute-start(bf16[63,1024]{1,0:T(8,128)(2,1)S(1)} %slice.42), channel_id=1, source_target_pairs={{4,0},{8,4},{12,8},{16,12},{20,16},{24,20},{28,24},{5,1},{9,5},{13... | collective-permute-start | bytes 387080 | tf_op jit(solution)/shard_map/ppermute | solution.py:23
  128.1 6.7 %copy-start.2 = (bf16[448,2048]{1,0:T(8,128)(2,1)S(1)}, bf16[448,2048]{1,0:T(8,128)(2,1)}, u32[]{:S(2)}) copy-start(bf16[448,2048]{1,0:T(8,128)(2,1)} %copy-done.1) | copy-start | bytes 5505028
  132.6 7.9 %collective-permute-start.1 = (bf16[63,1024]{1,0:T(8,128)(2,1)S(1)}, bf16[63,1024]{1,0:T(8,128)(2,1)S(1)}, u32[]{:S(2)}, u32[]{:S(2)}) collective-permute-start(bf16[63,1024]{1,0:T(8,128)(2,1)S(1)} %slice.44), channel_id=1, source_target_pairs={{0,4},{4,8},{8,12},{12,16},{16,20},{20,24},{24,28},{1,5},{5,9},{9,... | collective-permute-start | bytes 387080 | tf_op jit(solution)/shard_map/ppermute | solution.py:23
Sparse Core Ops, SparseCore 0:
  8.9 79.2 all-gather.1
